TPU v7x, 256 devices: a whole 4x4x8 slice. The times are simulated.
256 devices in a mesh: section: 16 (over x_lo, y, core), dp: 16 (over z, x_hi).
Axes of the slice: x: 4 (x_hi: 2, x_lo: 2; x = x_hi * 2 + x_lo), y: 4, z: 8, core: 2. Of those that a mesh axis runs over, the one named last changes fastest.
Arguments:
- activations: bfloat16 [16, 16, 64, 4096], P('section', 'dp'), may hold values from -6 to 6
- cotangents: bfloat16 [16, 16, 64, 14336], P('section', 'dp'), may hold values from -6 to 6
- mb_count: int32 [16, 16], P('section', 'dp'), may hold values from 2 to 4, as said below
- mb_size: int32 [16, 16, 4], P('section', 'dp'), may hold values from 8 to 16, as said below
- block_slot: int32 [16, 32], P('section'), may hold values from 0 to 31, as said below
- inv_blocks: bfloat16 [16, 32, 512, 512], P('section', 'dp'), may hold values from -1.5 to 1.5
Outputs:
- preconditioned: bfloat16 [16, 32, 512, 2048], P('section', 'dp')
- output_stats: bfloat16 [16, 32, 512, 256], P('section', 'dp')
- input_stats: float32 [16, 2048, 512], P('section', 'dp')
Inputs may be any that keep to these rules, and one draw needn't show every extreme that they name: `mb_count`: A device's live microbatches are its first slots; some device uses all 4. `mb_size`: some slot of some device is full. `block_slot`: on each section the first 28 entries are the slots of the hidden blocks and the next 4 those of the input blocks of the section's half; all distinct; slot q lies on dp device q // 2; the last slot is always taken.
All inputs are finite; a program needn't handle non-finite values.
Results may differ from a plain program's by a relative error of at most 0.015.
Values may be sent and summed in bfloat16 or wider, within the bound.
No kernel may reach another device: no remote copies, remote signals or barrier semaphores. Data moves between devices by JAX's collectives and lax.ppermute only.
A program may use at most 128 MiB of HBM per device.

v0:
```python
import jax
import jax.numpy as jnp
from jax import lax
from jax.sharding import PartitionSpec as P

MB = 4


def partner(value, axis, bit):
    mask = 2**bit
    pairs = [(source, source ^ mask) for source in range(lax.axis_size(axis))]
    return lax.ppermute(value, axis, pairs)


def from_root(block, axis, source):
    block = jnp.where(lax.axis_index(axis) == source, block, jnp.zeros_like(block))
    return lax.psum(block, axis)


def live_mask(count_live, sizes, rows_total, per_slot):
    index = jnp.arange(rows_total, dtype=jnp.int32)
    group = index // per_slot
    within = index % per_slot
    slot_ids = jnp.arange(sizes.shape[0], dtype=jnp.int32)
    picked = jnp.sum(jnp.where(group[:, None] == slot_ids[None, :], sizes[None, :], 0), axis=1)
    return (group < count_live) & (within < picked)


def contract_rows(first_mat, second_mat):
    return lax.dot_general(
        first_mat, second_mat, (((0,), (0,)), ((), ())), preferred_element_type=jnp.float32
    )


def gram_rows(matrix, row_count, block):
    pieces = []
    for piece_index in range(row_count // block):
        base_cols = lax.dynamic_slice_in_dim(matrix, piece_index * block, block, 1)
        pieces.append(contract_rows(base_cols, base_cols))
    return jnp.concatenate(pieces, axis=0)


def local(activations, cotangents, mb_count, mb_size, block_slot, inv_blocks):
    token_rows = activations.shape[2]
    width = activations.shape[3]
    hidden_width = cotangents.shape[3]
    block = inv_blocks.shape[2]
    slots_here = inv_blocks.shape[1]
    half_width = width // 2
    half_block = block // 2
    hidden_blocks = hidden_width // block
    input_blocks = half_width // block
    section_count = lax.axis_size("section")
    dp_count = lax.axis_size("dp")
    section_id = lax.axis_index("section")
    dp_id = lax.axis_index("dp")
    half_index = (section_id >= section_count // 2).astype(jnp.int32)
    zero_bf = jnp.zeros((), jnp.bfloat16)
    live_rows = live_mask(mb_count[0, 0], mb_size[0, 0], token_rows, token_rows // MB)
    own_x = jnp.where(live_rows[:, None], activations[0, 0], zero_bf)
    own_g = jnp.where(live_rows[:, None], cotangents[0, 0], zero_bf)
    own_cols = lax.dynamic_slice_in_dim(own_x, half_index * half_width, half_width, 1)
    sent_cols = lax.dynamic_slice_in_dim(own_x, (1 - half_index) * half_width, half_width, 1)
    bit_total = section_count.bit_length() - 1
    bit_order = list(range(bit_total))
    moving = (sent_cols, own_g)
    for bit_number in bit_order:
        moving = partner((moving[0], moving[1]), "section", bit_number)
    tokens_x = jnp.concatenate([own_cols, moving[0]], axis=0)
    tokens_g = jnp.concatenate([own_g, moving[1]], axis=0)
    pair_count = tokens_x.shape[0]
    layer_total = section_count // 2
    layer_index = jnp.minimum(section_id, section_count - 1 - section_id)
    layer_ids = jnp.arange(layer_total, dtype=jnp.int32)
    own_count = jnp.sum(live_rows.astype(jnp.int32))
    per_layer = jnp.where(layer_ids == layer_index, own_count, 0)
    layer_counts = lax.psum(per_layer, ("section", "dp"))
    token_total = jnp.sum(jnp.where(layer_ids == layer_index, layer_counts, 0)).astype(jnp.float32)
    slot_table = block_slot[0]
    hidden_table = slot_table[:hidden_blocks]
    input_table = slot_table[hidden_blocks:]
    hidden_ids = jnp.arange(hidden_blocks, dtype=jnp.int32)
    every_slot = jnp.arange(dp_count * slots_here, dtype=jnp.int32)
    slot_matches = hidden_table[None, :] == every_slot[:, None]
    slot_used = jnp.any(slot_matches, axis=1)
    block_pick = jnp.sum(jnp.where(slot_matches, hidden_ids[None, :], 0), axis=1)
    g_blocks = tokens_g.reshape(pair_count, hidden_blocks, block)
    outgoing = jnp.take(g_blocks, block_pick, axis=1)
    outgoing = jnp.where(slot_used[None, :, None], outgoing, zero_bf)
    routed = lax.all_to_all(outgoing, "dp", split_axis=1, concat_axis=0, tiled=True)
    routed_half = lax.dynamic_slice_in_dim(routed, half_index * half_block, half_block, 2)
    out_sum = jnp.einsum("rtb,rtc->tbc", routed, routed_half, preferred_element_type=jnp.float32)
    output_stats = (out_sum / token_total).astype(jnp.bfloat16)
    gram_count = half_width // dp_count
    scattered = lax.psum_scatter(
        gram_rows(tokens_x, gram_count * lax.axis_size("dp"), block).astype(jnp.bfloat16),
        "dp",
        scatter_dimension=0,
        tiled=True,
    ).astype(jnp.float32)
    input_stats = scattered / token_total
    grad_slot = (
        jnp.einsum(
            "rtb,rc->tbc",
            routed,
            lax.all_gather(tokens_x, "dp", axis=0, tiled=True),
            preferred_element_type=jnp.float32,
        )
        / token_total
    ).astype(jnp.bfloat16)
    local_blocks = inv_blocks[0]
    my_slots = dp_id * slots_here + jnp.arange(slots_here, dtype=jnp.int32)
    received = []
    for block_index in range(input_blocks):
        slot_number = input_table[block_index]
        owner = slot_number // slots_here
        held = lax.dynamic_index_in_dim(local_blocks, slot_number % slots_here, 0, keepdims=False)
        received.append(from_root(held, "dp", owner))
    a_inverse = jnp.stack(received)
    left = jnp.einsum(
        "qij,qjc->qic", local_blocks, grad_slot, preferred_element_type=jnp.float32
    ).astype(jnp.bfloat16)
    left = left.reshape(slots_here, block, input_blocks, block)
    scaled = jnp.einsum(
        "qikj,kjc->qikc", left, a_inverse, preferred_element_type=jnp.float32
    ).astype(jnp.bfloat16)
    scaled = scaled.reshape(slots_here, block, half_width)
    used_here = jnp.any(hidden_table[None, :] == my_slots[:, None], axis=1)
    scaled = jnp.where(used_here[:, None, None], scaled, zero_bf)
    return (scaled[None], output_stats[None], input_stats[None])


def solution(mesh):
    in_specs = (
        P("section", "dp", None, None),
        P("section", "dp", None, None),
        P("section", "dp"),
        P("section", "dp", None),
        P("section", None),
        P("section", "dp", None, None),
    )
    out_specs = (
        P("section", "dp", None, None),
        P("section", "dp", None, None),
        P("section", "dp", None),
    )
    return jax.shard_map(local, mesh=mesh, in_specs=in_specs, out_specs=out_specs, check_vma=False)
```

profile of v0, /device:TPU:16, one launch (start us, length us, event | category | flops | bytes accessed | tf_op | source)
XLA Modules:
  0.0 614.1 jit_solution(12101574751945445238)
XLA Ops:
  13.4 7.1 %collective-permute-done.5 = bf16[64,2048]{1,0:T(8,128)(2,1)S(1)} collective-permute-done((bf16[64,2048]{1,0:T(8,128)(2,1)S(1)}, bf16[64,2048]{1,0:T(8,128)(2,1)S(1)}, u32[]{:S(2)}, u32[]{:S(2)}) %collective-permute-start.5) | collective-permute-done | bytes 262176 | tf_op jit(solution)/shard_map/ppermute | solution.py:12
  22.5 7.0 %collective-permute-done.6 = bf16[64,2048]{1,0:T(8,128)(2,1)S(1)} collective-permute-done((bf16[64,2048]{1,0:T(8,128)(2,1)S(1)}, bf16[64,2048]{1,0:T(8,128)(2,1)S(1)}, u32[]{:S(2)}, u32[]{:S(2)}) %collective-permute-start.6) | collective-permute-done | bytes 262176 | tf_op jit(solution)/shard_map/ppermute | solution.py:12
  31.0 4.5 copy.44
  38.9 3.5 bitcast_select_fusion.1
  42.3 3.3 copy.45
  46.7 3.0 collective-permute-done
  51.0 41.0 %collective-permute-done.1 = bf16[64,14336]{1,0:T(8,128)(2,1)S(1)} collective-permute-done((bf16[64,14336]{1,0:T(8,128)(2,1)}, bf16[64,14336]{1,0:T(8,128)(2,1)S(1)}, u32[]{:S(2)}, u32[]{:S(2)}) %collective-permute-start.1) | collective-permute-done | bytes 1835040 | tf_op jit(solution)/shard_map/ppermute | solution.py:12
  94.0 40.8 %collective-permute-done.2 = bf16[64,14336]{1,0:T(8,128)(2,1)S(1)} collective-permute-done((bf16[64,14336]{1,0:T(8,128)(2,1)S(1)}, bf16[64,14336]{1,0:T(8,128)(2,1)S(1)}, u32[]{:S(2)}, u32[]{:S(2)}) %collective-permute-start.2) | collective-permute-done | bytes 1835040 | tf_op jit(solution)/shard_map/ppermute | solution.py:12
  136.6 41.4 %collective-permute-done.3 = bf16[64,14336]{1,0:T(8,128)(2,1)S(1)} collective-permute-done((bf16[64,14336]{1,0:T(8,128)(2,1)S(1)}, bf16[64,14336]{1,0:T(8,128)(2,1)S(1)}, u32[]{:S(2)}, u32[]{:S(2)}) %collective-permute-start.3) | collective-permute-done | bytes 1835040 | tf_op jit(solution)/shard_map/ppermute | solution.py:12
  178.0 3.0 copy.46
  181.0 5.4 pad_maximum_fusion
  186.4 5.9 copy.47
  192.3 4.9 gather_fusion
  197.2 4.7 select_bitcast_fusion
  201.9 12.2 %all-to-all-start = ((bf16[128,32,512]{2,0,1:T(8,128)(2,1)}), bf16[128,32,512]{2,0,1:T(8,128)(2,1)}, u32[]{:S(2)}, u32[]{:S(2)}) async-start(bf16[128,32,512]{2,0,1:T(8,128)(2,1)} %select_bitcast_fusion), calls=%async_computation | async-start | bytes 8388608 | tf_op jit(solution)/shard_map/all_to_all | solution.py:90
  230.8 164.1 %psum.39 = s32[8]{0:T(128)S(1)} all-reduce(s32[8]{0:T(128)S(1)} %compare_select_fusion.3), channel_id=1, replica_groups=mesh['section'=16,'dp'=16] {'section','dp'}, use_global_device_ids=true, to_apply=%region_9.10 | all-reduce | flops 8 | bytes 64 | tf_op jit(solution)/shard_map/psum | solution.py:77
  398.0 8.0 %copy.48 = bf16[16,128,2,512]{1,0,3,2:T(8,128)(2,1)} copy(bf16[16,128,2,512]{3,1,2,0:T(8,128)(2,1)} %bitcast.19) | data formatting | bytes 8388608 | tf_op jit(solution)/shard_map/all_to_all | solution.py:90
  406.0 7.3 %all_to_all.16 = bf16[2048,2,512]{0,2,1:T(8,128)(2,1)} reshape(bf16[16,128,2,512]{1,0,3,2:T(8,128)(2,1)} %copy.48) | data formatting | bytes 8388608 | tf_op jit(solution)/shard_map/all_to_all | solution.py:90
  413.3 5.0 fusion.22
  418.3 7.5 %all-gather.2.cloned.1.call-done = bf16[2048,2048]{1,0:T(8,128)(2,1)} async-done(((bf16[128,2048]{1,0:T(8,128)(2,1)}), bf16[2048,2048]{1,0:T(8,128)(2,1)}) %all-gather.2.cloned.1.call-update) | async-done | bytes 8388624 | tf_op jit(solution)/shard_map/all_gather | solution.py:106
  425.8 16.0 %convolution_convert_fusion = bf16[2,2048,512]{2,1,0:T(8,128)(2,1)} fusion(bf16[2048,2,512]{0,2,1:T(8,128)(2,1)} %all_to_all.16, bf16[2048,2048]{1,0:T(8,128)(2,1)} %all-gather.2.cloned.1.call-done, f32[]{:T(128)S(6)} %convert_element_type.33, bf16[1,2,512,512]{3,2,1,0:T(8,128)(2,1)S(1)} %copy-done), kind=kOutput, calls=%fused_computation.9 | convolution fusion | flops 10743709696 | bytes 17825796 | tf_op jit(solution)/shard_map/qij,qjc->qic/dot_general | solution.py:120
  441.7 151.6 %all-reduce.3.cloned.1.call-done = (bf16[1,512,512]{1,2,0:T(8,128)(2,1)}, bf16[1,512,512]{1,2,0:T(8,128)(2,1)}, bf16[1,512,512]{1,2,0:T(8,128)(2,1)}, bf16[1,512,512]{1,2,0:T(8,128)(2,1)}) async-done(((bf16[1,512,512]{1,2,0:T(8,128)(2,1)}, bf16[1,512,512]{1,2,0:T(8,128)(2,1)}, bf16[1,512,512]{1,2,0:T(8,128)(2,1)}, bf16[1,512,512]{1,2,0:T(8,128)(2,1)}), (bf16[1,512,512]{1,2,0:T(8,128)(2,1)}, ...) | async-done | bytes 2097168 | tf_op jit(solution)/shard_map/psum | solution.py:17
  593.3 5.2 convert_bitcast_fusion
  601.4 6.2 %copy.53 = bf16[1,2,512,2048]{3,2,1,0:T(8,128)(2,1)} copy(bf16[1,2,512,2048]{2,3,1,0:T(8,128)(2,1)} %bitcast_select_fusion) | data formatting | bytes 8388608
  (54 shorter events, 30.1 us)
Async XLA Ops:
  7.2 389.2 %reduce-scatter.2.cloned.1.call-start = ((), (), s32[]{:S(2)}) async-start(), calls=%async_computation.3 | async-start | bytes 2228224 | tf_op jit(solution)/shard_map/reduce_scatter | solution.py:95
  10.5 1.6 collective-permute-start.4
  12.1 8.3 %collective-permute-start.5 = (bf16[64,2048]{1,0:T(8,128)(2,1)S(1)}, bf16[64,2048]{1,0:T(8,128)(2,1)S(1)}, u32[]{:S(2)}, u32[]{:S(2)}) collective-permute-start(bf16[64,2048]{1,0:T(8,128)(2,1)S(1)} %collective-permute-done.4), channel_id=1, source_target_pairs={{0,32},{16,48},{32,0},{48,16},{64,96},{80,112},{96,64},{112,80},{1... | collective-permute-start | bytes 786440 | tf_op jit(solution)/shard_map/ppermute | solution.py:12
  20.5 9.0 %collective-permute-start.6 = (bf16[64,2048]{1,0:T(8,128)(2,1)S(1)}, bf16[64,2048]{1,0:T(8,128)(2,1)S(1)}, u32[]{:S(2)}, u32[]{:S(2)}) collective-permute-start(bf16[64,2048]{1,0:T(8,128)(2,1)S(1)} %collective-permute-done.5), channel_id=1, source_target_pairs={{0,64},{16,80},{32,96},{48,112},{64,0},{80,16},{96,32},{112,48},{1... | collective-permute-start | bytes 786440 | tf_op jit(solution)/shard_map/ppermute | solution.py:12
  29.5 6.6 %collective-permute-start.7 = (bf16[64,2048]{1,0:T(8,128)(2,1)S(1)}, bf16[64,2048]{1,0:T(8,128)(2,1)S(1)}, u32[]{:S(2)}, u32[]{:S(2)}) collective-permute-start(bf16[64,2048]{1,0:T(8,128)(2,1)S(1)} %collective-permute-done.6), channel_id=1, source_target_pairs={{0,128},{16,144},{32,160},{48,176},{64,192},{80,208},{96,224},{112... | collective-permute-start | bytes 786440 | tf_op jit(solution)/shard_map/ppermute | solution.py:12
  38.8 387.0 %all-gather.2.cloned.1.call-start = ((), (), s32[]{:S(2)}) async-start(), calls=%async_computation.2 | async-start | bytes 8912896 | tf_op jit(solution)/shard_map/all_gather | solution.py:106
  42.3 93.9 %copy-start.1 = (s32[1,32]{1,0:T(1,128)S(1)}, s32[1,32]{1,0:T(1,128)}, u32[]{:S(2)}) copy-start(s32[1,32]{1,0:T(1,128)} %param.10) | copy-start | bytes 388
  45.7 4.0 collective-permute-start
  49.7 42.3 %collective-permute-start.1 = (bf16[64,14336]{1,0:T(8,128)(2,1)}, bf16[64,14336]{1,0:T(8,128)(2,1)S(1)}, u32[]{:S(2)}, u32[]{:S(2)}) collective-permute-start(bf16[64,14336]{1,0:T(8,128)(2,1)} %collective-permute-done), channel_id=1, source_target_pairs={{0,32},{16,48},{32,0},{48,16},{64,96},{80,112},{96,64},{112,80},{1... | collective-permute-start | bytes 5505032 | tf_op jit(solution)/shard_map/ppermute | solution.py:12
  92.0 42.8 %collective-permute-start.2 = (bf16[64,14336]{1,0:T(8,128)(2,1)S(1)}, bf16[64,14336]{1,0:T(8,128)(2,1)S(1)}, u32[]{:S(2)}, u32[]{:S(2)}) collective-permute-start(bf16[64,14336]{1,0:T(8,128)(2,1)S(1)} %collective-permute-done.1), channel_id=1, source_target_pairs={{0,64},{16,80},{32,96},{48,112},{64,0},{80,16},{96,32},{112,48},{1... | collective-permute-start | bytes 5505032 | tf_op jit(solution)/shard_map/ppermute | solution.py:12
  134.8 43.2 %collective-permute-start.3 = (bf16[64,14336]{1,0:T(8,128)(2,1)S(1)}, bf16[64,14336]{1,0:T(8,128)(2,1)S(1)}, u32[]{:S(2)}, u32[]{:S(2)}) collective-permute-start(bf16[64,14336]{1,0:T(8,128)(2,1)S(1)} %collective-permute-done.2), channel_id=1, source_target_pairs={{0,128},{16,144},{32,160},{48,176},{64,192},{80,208},{96,224},{112... | collective-permute-start | bytes 5505032 | tf_op jit(solution)/shard_map/ppermute | solution.py:12
  201.9 23.1 %copy-start = (bf16[1,2,512,512]{3,2,1,0:T(8,128)(2,1)S(1)}, bf16[1,2,512,512]{3,2,1,0:T(8,128)(2,1)}, u32[]{:S(2)}) copy-start(bf16[1,2,512,512]{3,2,1,0:T(8,128)(2,1)} %param.11) | copy-start | bytes 3145732
  201.9 196.1 %all-to-all-start = ((bf16[128,32,512]{2,0,1:T(8,128)(2,1)}), bf16[128,32,512]{2,0,1:T(8,128)(2,1)}, u32[]{:S(2)}, u32[]{:S(2)}) async-start(bf16[128,32,512]{2,0,1:T(8,128)(2,1)} %select_bitcast_fusion), calls=%async_computation | async-start | bytes 8388608 | tf_op jit(solution)/shard_map/all_to_all | solution.py:90
  214.1 379.3 %all-reduce.3.cloned.1.call-start = ((), (), s32[]{:S(2)}) async-start(), calls=%async_computation.4 | async-start | bytes 4194304 | tf_op jit(solution)/shard_map/psum | solution.py:17
Sparse Core Ops, SparseCore 0:
  38.9 221.6 reduce-scatter.1
  263.3 162.4 all-gather.1
  428.7 164.6 all-reduce.2
where the time goes:
time: 615 us; the launch traced here: 614 us
  waiting for transfers between devices  301 us (49%)
  blocking collectives  164 us (27%)
  local copies, waits for them, and re-layouts  47 us (8%)
  matrix products  27.4 us (4%)
  other arithmetic  26.4 us (4%)
  between operations  25.6 us (4%)
  starting transfers between devices  22.2 us (4%)
    psum x1, blocking collectives, local(): layer_counts = lax.psum(per_layer, ('section', 'dp'))  164 us
    psum x1, waiting for transfers between devices, from_root(): return lax.psum(block, axis)  152 us
    ppermute x8, waiting for transfers between devices, partner(): return lax.ppermute(value, axis, pairs)  142 us
    dot_general x1, matrix products, local(): jnp.einsum('qij,qjc->qic', local_blocks, grad_slot, preferred_element_typ...  16 us
    all_to_all x2, local copies, waits for them, and re-layouts, local(): lax.all_to_all(outgoing, 'dp', split_axis=1, concat_axis=0, tiled=True)  15.3 us
    unnamed x10, local copies, waits for them, and re-layouts  12.6 us
  transfers between devices with their start and end apart: 12, of which 10 were waited for; matrix products, arithmetic and copies ran while one was open for 12% of the time, Pallas kernels for 0%

commit v1 on v0

v1 whole, which is shorter than its diff:
```python
import functools

import jax
import jax.numpy as jnp
from jax import lax
from jax.experimental import pallas as pl
from jax.experimental.pallas import tpu as pltpu
from jax.sharding import PartitionSpec as P

MB = 4
VMEM_BYTES = 56 * 1024 * 1024


def z_step(value, step):
    count = lax.axis_size("dp")
    pairs = [(d, (d + 2 * step) % count) for d in range(count)]
    return lax.ppermute(value, "dp", pairs)


def x_swap(value):
    count = lax.axis_size("dp")
    return lax.ppermute(value, "dp", [(d, d ^ 1) for d in range(count)])


def ring_start(start):
    return z_step(start, 1), z_step(start, -1)


def ring_start_pair(up, down):
    return z_step(up, 1), z_step(down, -1)


def ring_end(up, down):
    cut = up.shape[0] // 2
    return z_step(up[:cut], 1), z_step(down[cut:], -1)


def live_mask(count_live, sizes, rows_total, per_slot):
    index = jnp.arange(rows_total, dtype=jnp.int32)
    group = index // per_slot
    within = index % per_slot
    slot_ids = jnp.arange(sizes.shape[0], dtype=jnp.int32)
    picked = jnp.sum(jnp.where(group[:, None] == slot_ids[None, :], sizes[None, :], 0), axis=1)
    return (group < count_live) & (within < picked)


def contract_rows(first_mat, second_mat):
    return lax.dot_general(
        first_mat, second_mat, (((0,), (0,)), ((), ())), preferred_element_type=jnp.float32
    )


def route_kernel(slots_here, pick, limit, g_ref, out_ref):
    rows, _ = g_ref.shape
    dests, _, block = out_ref.shape
    per = rows // MB
    within = lax.broadcasted_iota(jnp.int32, (per, block), 0)
    keep = [within < limit[m] for m in range(MB)]

    @pl.loop(0, dests)
    def _(dest):
        for t in range(slots_here):
            number = pick[dest * slots_here + t]
            start = pl.multiple_of(number * block, block)
            for m in range(MB):
                part = g_ref[pl.ds(m * per, per), pl.ds(start, block)]
                part = jnp.where(keep[m], part, jnp.zeros_like(part))
                out_ref[dest, pl.ds(t * rows + m * per, per), :] = part


def route(pick, limit, g_rows, dests, slots_here, block):
    vmem = pl.BlockSpec(memory_space=pltpu.VMEM)
    smem = pl.BlockSpec(memory_space=pltpu.SMEM)
    return pl.pallas_call(
        functools.partial(route_kernel, slots_here),
        out_shape=jax.ShapeDtypeStruct((dests, slots_here * g_rows.shape[0], block), jnp.bfloat16),
        in_specs=[smem, smem, vmem],
        out_specs=vmem,
        compiler_params=pltpu.CompilerParams(vmem_limit_bytes=VMEM_BYTES),
        cost_estimate=pl.CostEstimate(flops=0, bytes_accessed=8 * 2**20, transcendentals=0),
    )(pick, limit, g_rows)


def pack_routed(rows, source, routed_ref, packed, turned):
    for t in range(turned.shape[0]):
        for n in range(routed_ref.shape[0]):
            packed[t, pl.ds(n * rows, rows), :] = routed_ref[source[n], pl.ds(t * rows, rows), :]
        turned[t] = packed[t].T


def half_columns(packed, t, half, half_block):
    return packed[t, :, pl.ds(pl.multiple_of(half * half_block, half_block), half_block)]


def gram_here(place, xs, width):
    cols = xs[:, pl.ds(pl.multiple_of(place[3] * width, width), width)]
    return jnp.dot(cols.T, xs[...], preferred_element_type=jnp.float32)


def ring_rows(shards, first, count):
    picked = []
    for d in range(4):
        picked.append([(shards[d], first, count)])
    top, bottom = shards[4], shards[5]
    cut = top.shape[0]
    upper = min(max(cut - first, 0), count)
    parts = []
    if upper:
        parts.append((top, first, upper))
    if upper < count:
        parts.append((bottom, first + upper - cut, count - upper))
    picked.append(parts)
    for d in (6, 7, 8):
        picked.append([(shards[d], first, count)])
    return picked


def first_kernel(rows, held, source, place, routed_ref, *refs):
    shards, (acc_ref, stat_ref, gram_ref, packed, turned, xs) = refs[:9], refs[9:]
    k = pl.program_id(0)

    @pl.when(k == 0)
    def _():
        pack_routed(rows, source, routed_ref, packed, turned)
        for t in range(turned.shape[0]):
            cols = half_columns(packed, t, place[0], stat_ref.shape[2])
            stat_ref[t] = jnp.dot(turned[t], cols, preferred_element_type=jnp.float32)

    at = 0
    mine, other = ring_rows(shards, 0, rows), ring_rows(shards, held, rows)
    for d in range(8):
        for ref, start, count in mine[d] + other[d]:
            xs[pl.ds(at, count), :] = ref[pl.ds(start, count), :]
            at += count
    for t in range(turned.shape[0]):
        acc_ref[t] = jnp.dot(turned[t], xs[...], preferred_element_type=jnp.float32)

    @pl.when(k == place[2])
    def _():
        gram_ref[...] = gram_here(place, xs, gram_ref.shape[0])


def column_spec(array, block):
    return pl.BlockSpec((array.shape[0], block), lambda k: (0, k))


def first_part(source, place, routed, shards, rows, held, slots_here, block):
    width = shards[0].shape[1]
    tokens = routed.shape[0] * rows
    gram_rows = width // routed.shape[0]
    vmem = pl.BlockSpec(memory_space=pltpu.VMEM)
    smem = pl.BlockSpec(memory_space=pltpu.SMEM)
    flops = 2 * slots_here * block * tokens * (width + block // 2)
    return pl.pallas_call(
        functools.partial(first_kernel, rows, held),
        grid=(width // block,),
        out_shape=(
            jax.ShapeDtypeStruct((slots_here, block, width), jnp.float32),
            jax.ShapeDtypeStruct((slots_here, block, block // 2), jnp.float32),
            jax.ShapeDtypeStruct((gram_rows, block), jnp.float32),
        ),
        in_specs=[smem, smem, vmem] + [column_spec(s, block) for s in shards],
        out_specs=(
            pl.BlockSpec((slots_here, block, block), lambda k: (0, 0, k)),
            pl.BlockSpec((slots_here, block, block // 2), lambda k: (0, 0, 0)),
            pl.BlockSpec((gram_rows, block), lambda k: (0, 0)),
        ),
        scratch_shapes=[
            pltpu.VMEM((slots_here, tokens, block), jnp.bfloat16),
            pltpu.VMEM((slots_here, block, tokens), jnp.bfloat16),
            pltpu.VMEM((tokens, block), jnp.bfloat16),
        ],
        compiler_params=pltpu.CompilerParams(vmem_limit_bytes=VMEM_BYTES),
        cost_estimate=pl.CostEstimate(flops=flops, bytes_accessed=16 * 2**20, transcendentals=0),
    )(source, place, routed, *shards)


def last_kernel(rows, first_late, source, place, used, scale, routed_ref, *refs):
    shards, swapped = refs[:9], refs[9:13]
    acc_ref, stat1_ref, gram1_ref, inv_ref, a_ref, out_ref, stat_ref, gram_ref, packed, turned, xs = refs[13:]
    k = pl.program_id(0)
    per_token = scale[0]

    @pl.when(k == 0)
    def _():
        pack_routed(rows, source, routed_ref, packed, turned)
        for t in range(turned.shape[0]):
            cols = half_columns(packed, t, place[0], stat_ref.shape[2])
            stat = stat1_ref[t] + jnp.dot(turned[t], cols, preferred_element_type=jnp.float32)
            stat_ref[t] = jnp.where(used[t] > 0, stat * per_token, 0.0).astype(stat_ref.dtype)

    one, two, three, four = swapped
    late = four.shape[0]
    partner = [(one, 0), (one, 1), (two, 0), (three, 0), (four, 0), (three, 1), (two, 1), (one, 2)]
    mine = ring_rows(shards, first_late, rows)
    at = 0
    for d in range(8):
        ref, number = partner[d]
        for ref, start, count in mine[d] + [(ref, number * late, rows)]:
            xs[pl.ds(at, count), :] = ref[pl.ds(start, count), :]
            at += count

    for t in range(turned.shape[0]):
        grad = acc_ref[t] + jnp.dot(turned[t], xs[...], preferred_element_type=jnp.float32)
        grad = (grad * per_token).astype(jnp.bfloat16)
        left = jnp.dot(inv_ref[t], grad, preferred_element_type=jnp.float32).astype(jnp.bfloat16)
        scaled = jnp.dot(left, a_ref[0], preferred_element_type=jnp.float32)
        out_ref[t] = jnp.where(used[t] > 0, scaled, 0.0).astype(out_ref.dtype)

    @pl.when(k == place[2])
    def _():
        gram_ref[...] = (gram1_ref[...] + gram_here(place, xs, gram_ref.shape[0])) * per_token


def last_part(source, place, used, scale, routed, shards, swapped, acc, stat1, gram1, inverses, a_inverse, rows, first_late):
    width = acc.shape[2]
    slots_here, block = inverses.shape[:2]
    tokens = routed.shape[0] * rows
    vmem = pl.BlockSpec(memory_space=pltpu.VMEM)
    smem = pl.BlockSpec(memory_space=pltpu.SMEM)
    flops = 2 * slots_here * block * width * (tokens + 2 * block)
    return pl.pallas_call(
        functools.partial(last_kernel, rows, first_late),
        grid=(width // block,),
        out_shape=(
            jax.ShapeDtypeStruct((slots_here, block, width), jnp.bfloat16),
            jax.ShapeDtypeStruct((slots_here, block, block // 2), jnp.bfloat16),
            jax.ShapeDtypeStruct(gram1.shape, jnp.float32),
        ),
        in_specs=[smem, smem, smem, smem, vmem]
        + [column_spec(s, block) for s in list(shards) + list(swapped)]
        + [
            pl.BlockSpec((slots_here, block, block), lambda k: (0, 0, k)), vmem, vmem, vmem,
            pl.BlockSpec((1, block, block), lambda k: (k, 0, 0)),
        ],
        out_specs=(
            pl.BlockSpec((slots_here, block, block), lambda k: (0, 0, k)),
            pl.BlockSpec((slots_here, block, block // 2), lambda k: (0, 0, 0)),
            pl.BlockSpec(gram1.shape, lambda k: (0, 0)),
        ),
        scratch_shapes=[
            pltpu.VMEM((slots_here, tokens, block), jnp.bfloat16),
            pltpu.VMEM((slots_here, block, tokens), jnp.bfloat16),
            pltpu.VMEM((tokens, block), jnp.bfloat16),
        ],
        compiler_params=pltpu.CompilerParams(vmem_limit_bytes=VMEM_BYTES),
        cost_estimate=pl.CostEstimate(flops=flops, bytes_accessed=24 * 2**20, transcendentals=0),
    )(source, place, used, scale, routed, *shards, *swapped, acc, stat1, gram1, inverses, a_inverse)


def local(activations, cotangents, mb_count, mb_size, block_slot, inv_blocks):
    rows = activations.shape[2]
    width = activations.shape[3]
    hidden_width = cotangents.shape[3]
    block = inv_blocks.shape[2]
    slots_here = inv_blocks.shape[1]
    half_width = width // 2
    hidden_blocks = hidden_width // block
    input_blocks = half_width // block
    section_count = lax.axis_size("section")
    dp_count = lax.axis_size("dp")
    section_id = lax.axis_index("section")
    dp_id = lax.axis_index("dp")
    half = (section_id >= section_count // 2).astype(jnp.int32)
    zero_bf = jnp.zeros((), jnp.bfloat16)
    mirror = [(s, section_count - 1 - s) for s in range(section_count)]

    x_all = activations[0, 0]
    g_raw = cotangents[0, 0]
    local_blocks = inv_blocks[0]
    meta = jnp.concatenate([mb_count[0], mb_size[0, 0]])
    meta_m = lax.ppermute(meta, "section", mirror)
    x_sent = lax.dynamic_slice_in_dim(x_all, (1 - half) * half_width, half_width, 1)
    x_m = lax.ppermute(x_sent, "section", mirror)
    g_m = lax.ppermute(g_raw, "section", mirror)

    def limits(numbers):
        return jnp.where(jnp.arange(MB, dtype=jnp.int32) < numbers[0], numbers[1:], 0)

    slot_table = block_slot[0]
    hidden_table = slot_table[:hidden_blocks]
    input_table = slot_table[hidden_blocks:]
    hidden_ids = jnp.arange(hidden_blocks, dtype=jnp.int32)
    every_slot = jnp.arange(dp_count * slots_here, dtype=jnp.int32)
    slot_matches = hidden_table[None, :] == every_slot[:, None]
    block_pick = jnp.sum(jnp.where(slot_matches, hidden_ids[None, :], 0), axis=1)
    my_slots = dp_id * slots_here + jnp.arange(slots_here, dtype=jnp.int32)
    used_here = jnp.any(hidden_table[None, :] == my_slots[:, None], axis=1).astype(jnp.int32)

    z_count = dp_count // 2
    z_here, x_here = dp_id // 2, lax.rem(dp_id, 2)

    out_own = route(block_pick, limits(meta), g_raw, dp_count, slots_here, block)

    live_own = live_mask(meta[0], meta[1:], rows, rows // MB)
    live_mir = live_mask(meta_m[0], meta_m[1:], rows, rows // MB)
    count = jnp.sum(live_own.astype(jnp.int32)) + jnp.sum(live_mir.astype(jnp.int32))
    x_own = lax.dynamic_slice_in_dim(x_all, half * half_width, half_width, 1)
    x_own = jnp.where(live_own[:, None], x_own, zero_bf)
    x_mir = jnp.where(live_mir[:, None], x_m, zero_bf)
    held = rows
    first_late = 2 * held
    start = jnp.concatenate([x_own, x_swap(x_own), x_mir], axis=0)

    half_block = block // 2
    piece = half_block // z_count
    kept = lax.dynamic_slice_in_dim(local_blocks, x_here * half_block, half_block, 1)
    given = lax.dynamic_slice_in_dim(local_blocks, (1 - x_here) * half_block, half_block, 1)
    near = jnp.concatenate([kept, x_swap(given)], axis=0)
    owner = input_table // slots_here
    near_index = jnp.where(owner % 2 == x_here, 0, slots_here) + input_table % slots_here
    part = jnp.where((owner // 2 == z_here)[:, None, None], jnp.take(near, near_index, axis=0), zero_bf)
    part = part.reshape(input_blocks, z_count, piece, block)

    def part_for(offset):
        return lax.dynamic_index_in_dim(part, lax.rem(z_here + offset + z_count, z_count), 1, keepdims=False)

    out_mir = route(block_pick, limits(meta_m), g_m, dp_count, slots_here, block)

    def late_swap(*parts):
        return x_swap(jnp.concatenate([part[first_late:] for part in parts], axis=0))

    up1, down1 = ring_start(start)
    sum_up, sum_down = z_step(part_for(4), 1), z_step(part_for(-3), -1)
    one = late_swap(start, up1, down1)
    up2, down2 = ring_start_pair(up1, down1)
    sum_up, sum_down = z_step(part_for(3) + sum_up, 1), z_step(part_for(-2) + sum_down, -1)
    two = late_swap(up2, down2)
    up3, down3 = ring_start_pair(up2, down2)
    sum_up, sum_down = z_step(part_for(2) + sum_up, 1), z_step(part_for(-1) + sum_down, -1)
    up3, down3, out_own = lax.optimization_barrier((up3, down3, out_own))
    in_own = lax.all_to_all(out_own, "dp", split_axis=0, concat_axis=0, tiled=True)
    three = late_swap(up3, down3)
    top4, bottom4 = ring_end(up3, down3)
    sum_up = z_step(part_for(1) + sum_up, 1)
    mine = (part_for(0) + sum_up + sum_down).reshape(input_blocks * piece, block)
    cut = top4.shape[0]
    opposite = jnp.concatenate([top4, bottom4], axis=0)[first_late:] if first_late < cut else bottom4[first_late - cut :]
    four = x_swap(opposite)
    shards = [start, up1, up2, up3, top4, bottom4, down3, down2, down1]

    in_mir = lax.all_to_all(out_mir, "dp", split_axis=0, concat_axis=0, tiled=True)

    counts = jnp.full((16, block), count.astype(jnp.bfloat16))
    a0 = jnp.concatenate([mine, counts], axis=0)
    a_up1, a_down1 = ring_start(a0)
    a_up2, a_down2 = ring_start_pair(a_up1, a_down1)
    a_up3, a_down3 = ring_start_pair(a_up2, a_down2)
    a_four = jnp.concatenate([z_step(a_up3[: a0.shape[0] // 2], 1), z_step(a_down3[a0.shape[0] // 2 :], -1)], axis=0)
    a_one = x_swap(jnp.concatenate([a0, a_up1, a_down1], axis=0)).reshape(3, -1, block)
    a_two = x_swap(jnp.concatenate([a_up2, a_down2], axis=0)).reshape(2, -1, block)
    a_three = x_swap(jnp.concatenate([a_up3, a_down3], axis=0)).reshape(2, -1, block)
    a_last = x_swap(a_four)
    near_parts = [a0, a_up1, a_up2, a_up3, a_four, a_down3, a_down2, a_down1]
    far_parts = [a_one[0], a_one[1], a_two[0], a_three[0], a_last, a_three[1], a_two[1], a_one[2]]

    z_from = lax.rem(z_here - jnp.arange(z_count, dtype=jnp.int32) + z_count, z_count)
    x_order = jnp.stack([x_here, 1 - x_here])
    source = (z_from[:, None] * 2 + x_order[None, :]).reshape(-1)
    per_block = dp_count // input_blocks
    place = jnp.stack([half, dp_id, dp_id // per_block, lax.rem(dp_id, per_block)]).astype(jnp.int32)

    swapped = [one, two, three, four]
    in_ring = jnp.stack([p for pair in zip(near_parts, far_parts) for p in pair])
    token_total = jnp.sum(in_ring[:, input_blocks * piece, 0].astype(jnp.float32)).reshape(1)
    in_ring = in_ring[:, : input_blocks * piece].reshape(dp_count, input_blocks, piece, block)
    ordered = (x_order[None, :] * z_count + z_from[:, None]).reshape(-1)
    matches = ordered[None, :] == jnp.arange(dp_count, dtype=jnp.int32)[:, None]
    ring_place = jnp.sum(jnp.where(matches, jnp.arange(dp_count, dtype=jnp.int32)[None, :], 0), axis=1)
    a_inverse = jnp.take(in_ring, ring_place, axis=0).transpose(1, 0, 2, 3).reshape(input_blocks, block, block)

    scale = 1.0 / token_total
    acc, stat1, gram1 = first_part(source, place, in_own, shards, rows, held, slots_here, block)
    preconditioned, output_stats, input_stats = last_part(
        source, place, used_here, scale, in_mir, shards, swapped, acc, stat1, gram1, local_blocks, a_inverse,
        rows, first_late,
    )
    return (preconditioned[None], output_stats[None], input_stats[None])


def solution(mesh):
    in_specs = (
        P("section", "dp", None, None),
        P("section", "dp", None, None),
        P("section", "dp"),
        P("section", "dp", None),
        P("section", None),
        P("section", "dp", None, None),
    )
    out_specs = (
        P("section", "dp", None, None),
        P("section", "dp", None, None),
        P("section", "dp", None),
    )
    return jax.shard_map(local, mesh=mesh, in_specs=in_specs, out_specs=out_specs, check_vma=False)
```

time: 615 us -> 283 us (0.46)
  waiting for transfers between devices: 301 us -> 129 us
  blocking collectives: 164 us -> 0 us
  starting transfers between devices: 22.2 us -> 74 us
  Pallas kernels: 0 us -> 34.6 us
  matrix products: 27.4 us -> 0 us
  local copies, waits for them, and re-layouts: 47 us -> 25 us
  between operations: 25.6 us -> 4.06 us
  other arithmetic: 26.4 us -> 13.3 us
    psum x1 -> x0, blocking collectives: 164 us -> none  [local(): layer_counts = lax.psum(per_layer, ('section', 'dp'))]
    psum x1 -> x0, waiting for transfers between devices: 152 us -> none  [from_root(): return lax.psum(block, axis)]
    ppermute x8 -> x36, starting transfers between devices: 9.88 us -> 64.4 us  [the longest x23 36.2 us: z_step(): return lax.ppermute(value, 'dp', pairs)]
    pallas_call x0 -> x4, Pallas kernels: none -> 34.6 us  [the longest x1 16.7 us: last_part(): pl.pallas_call(functools.partial(last_kernel, rows, first_late), grid=(wi...]
    dot_general x7 -> x0, matrix products: 27.4 us -> none  [the longest x1 16 us: local(): jnp.einsum('qij,qjc->qic', local_blocks, grad_slot, preferred_element_typ...]
    all_to_all x2 -> x0, local copies, waits for them, and re-layouts: 15.3 us -> none  [local(): lax.all_to_all(outgoing, 'dp', split_axis=1, concat_axis=0, tiled=True)]
    ppermute x8 -> x36, waiting for transfers between devices: 142 us -> 129 us  [the longest x23 115 us: z_step(): return lax.ppermute(value, 'dp', pairs)]
    select_n x6 -> x8, other arithmetic: 12.5 us -> 2.85 us  [the longest x2 1.13 us: limits(): jnp.where(jnp.arange(MB, dtype=jnp.int32) < numbers[0], numbers[1:], 0)]
  transfers between devices with their start and end apart: 12 -> 38, of which waited for: 10 -> 15; matrix products, arithmetic and copies ran while one was open for 12% -> 13% of each run, Pallas kernels for 0% -> 6%
where the time goes in v1:
time: 283 us; the launch traced here: 280 us
  waiting for transfers between devices  129 us (46%)
  starting transfers between devices  74 us (26%)
  Pallas kernels  34.6 us (12%)
  local copies, waits for them, and re-layouts  25 us (9%)
  other arithmetic  13.3 us (5%)
  between operations  4.06 us (1%)
    ppermute x23, waiting for transfers between devices, z_step(): return lax.ppermute(value, 'dp', pairs)  115 us
    ppermute x23, starting transfers between devices, z_step(): return lax.ppermute(value, 'dp', pairs)  36.2 us
    ppermute x10, starting transfers between devices, x_swap(): return lax.ppermute(value, 'dp', [(d, d ^ 1) for d in range(count)])  25.5 us
    pallas_call x1, Pallas kernels, last_part(): pl.pallas_call(functools.partial(last_kernel, rows, first_late), grid=(wi...  16.7 us
    ppermute x10, waiting for transfers between devices, x_swap(): return lax.ppermute(value, 'dp', [(d, d ^ 1) for d in range(count)])  13.8 us
    pallas_call x1, Pallas kernels, first_part(): pl.pallas_call(functools.partial(first_kernel, rows, held), grid=(width /...  11.7 us
    unnamed x34, local copies, waits for them, and re-layouts  7.68 us
    pallas_call x2, Pallas kernels, route(): pl.pallas_call(functools.partial(route_kernel, slots_here), out_shape=jax...  6.23 us
  transfers between devices with their start and end apart: 38, of which 15 were waited for; matrix products, arithmetic and copies ran while one was open for 13% of the time, Pallas kernels for 6%

profile of v1, /device:TPU:16, one launch (start us, length us, event | category | flops | bytes accessed | tf_op | source)
XLA Modules:
  0.0 280.5 jit_solution(12961985026431754124)
XLA Ops:
  13.0 7.8 %collective-permute-done.22 = bf16[64,2048]{1,0:T(8,128)(2,1)S(1)} collective-permute-done((bf16[64,2048]{1,0:T(8,128)(2,1)S(1)}, bf16[64,2048]{1,0:T(8,128)(2,1)S(1)}, u32[]{:S(2)}, u32[]{:S(2)}) %collective-permute-start.22) | collective-permute-done | bytes 262176 | tf_op jit(solution)/shard_map/ppermute | solution.py:22
  20.8 5.9 %collective-permute-start.27 = (bf16[192,2048]{1,0:T(8,128)(2,1)S(1)}, bf16[192,2048]{1,0:T(8,128)(2,1)}, u32[]{:S(2)}, u32[]{:S(2)}) collective-permute-start(bf16[192,2048]{1,0:T(8,128)(2,1)S(1)} %pad_maximum_fusion.1.refs_0_), channel_id=1, source_target_pairs={{0,14},{1,15},{2,0},{3,1},{4,2},{5,3},{6,4},{7,5},{8,6},{9,7},{10,... | collective-permute-start | bytes 2359304 | tf_op jit(solution)/shard_map/ppermute | solution.py:17
  28.0 15.0 %collective-permute-done.27.refs_8_ = bf16[192,2048]{1,0:T(8,128)(2,1)} collective-permute-done((bf16[192,2048]{1,0:T(8,128)(2,1)S(1)}, bf16[192,2048]{1,0:T(8,128)(2,1)}, u32[]{:S(2)}, u32[]{:S(2)}) %collective-permute-start.27) | collective-permute-done | bytes 786464 | tf_op jit(solution)/shard_map/ppermute | solution.py:17
  43.0 3.8 %collective-permute-start.28 = (bf16[192,2048]{1,0:T(8,128)(2,1)}, bf16[192,2048]{1,0:T(8,128)(2,1)}, u32[]{:S(2)}, u32[]{:S(2)}) collective-permute-start(bf16[192,2048]{1,0:T(8,128)(2,1)} %collective-permute-done.27.refs_8_), channel_id=1, source_target_pairs={{0,14},{1,15},{2,0},{3,1},{4,2},{5,3},{6,4},{7,5},{8,6},{9,7},{10,... | collective-permute-start | bytes 2359304 | tf_op jit(solution)/shard_map/ppermute | solution.py:17
  48.2 14.3 %collective-permute-done.28.refs_7_ = bf16[192,2048]{1,0:T(8,128)(2,1)} collective-permute-done((bf16[192,2048]{1,0:T(8,128)(2,1)}, bf16[192,2048]{1,0:T(8,128)(2,1)}, u32[]{:S(2)}, u32[]{:S(2)}) %collective-permute-start.28) | collective-permute-done | bytes 786464 | tf_op jit(solution)/shard_map/ppermute | solution.py:17
  62.4 3.7 %collective-permute-start.29 = (bf16[192,2048]{1,0:T(8,128)(2,1)}, bf16[192,2048]{1,0:T(8,128)(2,1)}, u32[]{:S(2)}, u32[]{:S(2)}) collective-permute-start(bf16[192,2048]{1,0:T(8,128)(2,1)} %collective-permute-done.28.refs_7_), channel_id=1, source_target_pairs={{0,14},{1,15},{2,0},{3,1},{4,2},{5,3},{6,4},{7,5},{8,6},{9,7},{10,... | collective-permute-start | bytes 2359304 | tf_op jit(solution)/shard_map/ppermute | solution.py:17
  70.5 10.4 %collective-permute-done.29.refs_6_ = bf16[192,2048]{1,0:T(8,128)(2,1)} collective-permute-done((bf16[192,2048]{1,0:T(8,128)(2,1)}, bf16[192,2048]{1,0:T(8,128)(2,1)}, u32[]{:S(2)}, u32[]{:S(2)}) %collective-permute-start.29) | collective-permute-done | bytes 786464 | tf_op jit(solution)/shard_map/ppermute | solution.py:17
  80.9 4.8 %collective-permute-done.26.refs_3_ = bf16[192,2048]{1,0:T(8,128)(2,1)} collective-permute-done((bf16[192,2048]{1,0:T(8,128)(2,1)}, bf16[192,2048]{1,0:T(8,128)(2,1)}, u32[]{:S(2)}, u32[]{:S(2)}) %collective-permute-start.26) | collective-permute-done | bytes 786464 | tf_op jit(solution)/shard_map/ppermute | solution.py:17
  85.7 4.4 %all-to-all-start.1 = ((bf16[16,128,512]{2,1,0:T(8,128)(2,1)}), bf16[16,128,512]{2,1,0:T(8,128)(2,1)}, u32[]{:S(2)}, u32[]{:S(2)}) async-start(bf16[16,128,512]{2,1,0:T(8,128)(2,1)} %shard_map.86), calls=%async_computation.1 | async-start | bytes 4194304 | tf_op jit(solution)/shard_map/all_to_all | solution.py:332
  93.8 43.3 %collective-permute-done.2 = bf16[4,32,512]{2,1,0:T(8,128)(2,1)S(1)} collective-permute-done((bf16[4,32,512]{2,1,0:T(8,128)(2,1)S(1)}, bf16[4,32,512]{2,1,0:T(8,128)(2,1)S(1)}, u32[]{:S(2)}, u32[]{:S(2)}) %collective-permute-start.2) | collective-permute-done | bytes 131104 | tf_op jit(solution)/shard_map/ppermute | solution.py:17
  137.2 6.2 %collective-permute-done.3 = bf16[4,32,512]{2,1,0:T(8,128)(2,1)S(1)} collective-permute-done((bf16[4,32,512]{2,1,0:T(8,128)(2,1)S(1)}, bf16[4,32,512]{2,1,0:T(8,128)(2,1)S(1)}, u32[]{:S(2)}, u32[]{:S(2)}) %collective-permute-start.3) | collective-permute-done | bytes 131104 | tf_op jit(solution)/shard_map/ppermute | solution.py:17
  148.7 3.5 %collective-permute-start.7 = (bf16[4,32,512]{2,1,0:T(8,128)(2,1)S(1)}, bf16[4,32,512]{2,1,0:T(8,128)(2,1)S(1)}, u32[]{:S(2)}, u32[]{:S(2)}) collective-permute-start(bf16[4,32,512]{2,1,0:T(8,128)(2,1)S(1)} %bitcast_add_fusion.1), channel_id=1, source_target_pairs={{0,14},{1,15},{2,0},{3,1},{4,2},{5,3},{6,4},{7,5},{8,6},{9,7},{10,... | collective-permute-start | bytes 393224 | tf_op jit(solution)/shard_map/ppermute | solution.py:17
  154.8 3.7 %collective-permute-start.10 = (bf16[144,512]{1,0:T(8,128)(2,1)S(1)}, bf16[144,512]{1,0:T(8,128)(2,1)S(1)}, u32[]{:S(2)}, u32[]{:S(2)}) collective-permute-start(bf16[144,512]{1,0:T(8,128)(2,1)S(1)} %concatenate.40), channel_id=1, source_target_pairs={{0,14},{1,15},{2,0},{3,1},{4,2},{5,3},{6,4},{7,5},{8,6},{9,7},{10,... | collective-permute-start | bytes 442376 | tf_op jit(solution)/shard_map/ppermute | solution.py:17
  162.4 3.2 %collective-permute-start.13 = (bf16[144,512]{1,0:T(8,128)(2,1)S(1)}, bf16[144,512]{1,0:T(8,128)(2,1)S(1)}, u32[]{:S(2)}, u32[]{:S(2)}) collective-permute-start(bf16[144,512]{1,0:T(8,128)(2,1)S(1)} %collective-permute-done.10), channel_id=1, source_target_pairs={{0,14},{1,15},{2,0},{3,1},{4,2},{5,3},{6,4},{7,5},{8,6},{9,7},{10,... | collective-permute-start | bytes 442376 | tf_op jit(solution)/shard_map/ppermute | solution.py:17
  169.7 3.2 %collective-permute-start.16 = (bf16[144,512]{1,0:T(8,128)(2,1)S(1)}, bf16[144,512]{1,0:T(8,128)(2,1)S(1)}, u32[]{:S(2)}, u32[]{:S(2)}) collective-permute-start(bf16[144,512]{1,0:T(8,128)(2,1)S(1)} %collective-permute-done.13), channel_id=1, source_target_pairs={{0,14},{1,15},{2,0},{3,1},{4,2},{5,3},{6,4},{7,5},{8,6},{9,7},{10,... | collective-permute-start | bytes 442376 | tf_op jit(solution)/shard_map/ppermute | solution.py:17
  178.9 4.8 %collective-permute-done.18 = bf16[72,512]{1,0:T(8,128)(2,1)S(1)} collective-permute-done((bf16[72,512]{1,0:T(8,128)(2,1)S(1)}, bf16[72,512]{1,0:T(8,128)(2,1)S(1)}, u32[]{:S(2)}, u32[]{:S(2)}) %collective-permute-start.18) | collective-permute-done | bytes 73760 | tf_op jit(solution)/shard_map/ppermute | solution.py:17
  184.3 3.7 %collective-permute-done.19 = bf16[72,512]{1,0:T(8,128)(2,1)S(1)} collective-permute-done((bf16[72,512]{1,0:T(8,128)(2,1)S(1)}, bf16[72,512]{1,0:T(8,128)(2,1)S(1)}, u32[]{:S(2)}, u32[]{:S(2)}) %collective-permute-start.19) | collective-permute-done | bytes 73760 | tf_op jit(solution)/shard_map/ppermute | solution.py:17
  190.2 6.0 %collective-permute-done.11 = bf16[432,512]{1,0:T(8,128)(2,1)S(1)} collective-permute-done((bf16[432,512]{1,0:T(8,128)(2,1)S(1)}, bf16[432,512]{1,0:T(8,128)(2,1)S(1)}, u32[]{:S(2)}, u32[]{:S(2)}) %collective-permute-start.11) | collective-permute-done | bytes 442400 | tf_op jit(solution)/shard_map/ppermute | solution.py:22
  196.2 4.0 %collective-permute-start.20 = (bf16[144,512]{1,0:T(8,128)(2,1)}, bf16[144,512]{1,0:T(8,128)(2,1)}, u32[]{:S(2)}, u32[]{:S(2)}) collective-permute-start(bf16[144,512]{1,0:T(8,128)(2,1)} %constant_dynamic-update-slice_fusion), channel_id=1, source_target_pairs={{0,1},{1,0},{2,3},{3,2},{4,5},{5,4},{6,7},{7,6},{8,9},{9,8},{10,11... | collective-permute-start | bytes 442376 | tf_op jit(solution)/shard_map/ppermute | solution.py:22
  203.4 5.2 %all-to-all-start = ((bf16[16,128,512]{2,1,0:T(8,128)(2,1)}), bf16[16,128,512]{2,1,0:T(8,128)(2,1)}, u32[]{:S(2)}, u32[]{:S(2)}) async-start(bf16[16,128,512]{2,1,0:T(8,128)(2,1)} %shard_map.85), calls=%async_computation | async-start | bytes 4194304 | tf_op jit(solution)/shard_map/all_to_all | solution.py:342
  212.4 3.4 %collective-permute-start.33 = (bf16[128,2048]{1,0:T(8,128)(2,1)}, bf16[128,2048]{1,0:T(8,128)(2,1)}, u32[]{:S(2)}, u32[]{:S(2)}) collective-permute-start(bf16[128,2048]{1,0:T(8,128)(2,1)} %pad_maximum_fusion.3), channel_id=1, source_target_pairs={{0,1},{1,0},{2,3},{3,2},{4,5},{5,4},{6,7},{7,6},{8,9},{9,8},{10,11... | collective-permute-start | bytes 1572872 | tf_op jit(solution)/shard_map/ppermute | solution.py:22
  239.2 9.0 %collective-permute-done.31.refs_5_ = bf16[96,2048]{1,0:T(8,128)(2,1)S(1)} collective-permute-done((bf16[96,2048]{1,0:T(8,128)(2,1)S(1)}, bf16[96,2048]{1,0:T(8,128)(2,1)S(1)}, u32[]{:S(2)}, u32[]{:S(2)}) %collective-permute-start.31) | collective-permute-done | bytes 393248 | tf_op jit(solution)/shard_map/ppermute | solution.py:17
  250.9 11.7 %shard_map.87 = (f32[2,512,2048]{2,1,0:T(8,128)}, f32[2,512,256]{2,1,0:T(8,128)}, f32[128,512]{1,0:T(8,128)}) custom-call(s32[16]{0:T(128)} %add.292.source, s32[4]{0:T(128)} %pad_add_fusion.1.place, bf16[16,128,512]{2,1,0:T(8,128)(2,1)} %all-to-all-done.1.routed_ref, bf16[192,2048]{1,0:T(8,128)(2,1)} %copy-done.2, ...), custom_call_target="tpu_custom_call" | custom-call | flops 4831838208 | bytes 16777216 | tf_op jit(solution)/shard_map/pallas_call | solution.py:154
  263.6 16.7 %shard_map.88 = (bf16[2,512,2048]{2,1,0:T(8,128)(2,1)}, bf16[2,512,256]{2,1,0:T(8,128)(2,1)}, f32[128,512]{1,0:T(8,128)}) custom-call(s32[16]{0:T(128)} %add.292.source, s32[4]{0:T(128)} %pad_add_fusion.1.place, s32[2]{0:T(128)} %convert_element_type.20.used, f32[1]{0:T(128)} %bitcast.42.scale, bf16[16,128,512]{2,1,0:T(8,128)(2,1)} %all-to-all-done.routed_ref, ...), custom_call_target="tpu_custom_call" | custom-call | flops 8589934592 | bytes 25165824 | tf_op jit(solution)/shard_map/pallas_call | solution.py:222
  (158 shorter events, 78.7 us)
Async XLA Ops:
  9.1 11.7 %collective-permute-start.22 = (bf16[64,2048]{1,0:T(8,128)(2,1)S(1)}, bf16[64,2048]{1,0:T(8,128)(2,1)S(1)}, u32[]{:S(2)}, u32[]{:S(2)}) collective-permute-start(bf16[64,2048]{1,0:T(8,128)(2,1)S(1)} %bitcast_select_fusion), channel_id=1, source_target_pairs={{0,1},{1,0},{2,3},{3,2},{4,5},{5,4},{6,7},{7,6},{8,9},{9,8},{10,11... | collective-permute-start | bytes 786440 | tf_op jit(solution)/shard_map/ppermute | solution.py:22
  20.8 22.2 %collective-permute-start.27 = (bf16[192,2048]{1,0:T(8,128)(2,1)S(1)}, bf16[192,2048]{1,0:T(8,128)(2,1)}, u32[]{:S(2)}, u32[]{:S(2)}) collective-permute-start(bf16[192,2048]{1,0:T(8,128)(2,1)S(1)} %pad_maximum_fusion.1.refs_0_), channel_id=1, source_target_pairs={{0,14},{1,15},{2,0},{3,1},{4,2},{5,3},{6,4},{7,5},{8,6},{9,7},{10,... | collective-permute-start | bytes 2359304 | tf_op jit(solution)/shard_map/ppermute | solution.py:17
  26.8 20.0 %collective-permute-start.24 = (bf16[192,2048]{1,0:T(8,128)(2,1)S(1)}, bf16[192,2048]{1,0:T(8,128)(2,1)}, u32[]{:S(2)}, u32[]{:S(2)}) collective-permute-start(bf16[192,2048]{1,0:T(8,128)(2,1)S(1)} %pad_maximum_fusion.1.refs_0_), channel_id=1, source_target_pairs={{0,2},{1,3},{2,4},{3,5},{4,6},{5,7},{6,8},{7,9},{8,10},{9,11},{10,... | collective-permute-start | bytes 2359304 | tf_op jit(solution)/shard_map/ppermute | solution.py:17
  26.8 42.5 %collective-permute-start = (bf16[2,256,512]{2,1,0:T(8,128)(2,1)S(1)}, bf16[2,256,512]{2,1,0:T(8,128)(2,1)S(1)}, u32[]{:S(2)}, u32[]{:S(2)}) collective-permute-start(bf16[2,256,512]{2,1,0:T(8,128)(2,1)S(1)} %get-tuple-element.36), channel_id=1, source_target_pairs={{0,1},{1,0},{2,3},{3,2},{4,5},{5,4},{6,7},{7,6},{8,9},{9,8},{10,11... | collective-permute-start | bytes 1572872 | tf_op jit(solution)/shard_map/ppermute | solution.py:22
  27.9 172.4 %collective-permute-start.21 = (bf16[64,14336]{1,0:T(8,128)(2,1)}, bf16[64,14336]{1,0:T(8,128)(2,1)}, u32[]{:S(2)}, u32[]{:S(2)}) collective-permute-start(bf16[64,14336]{1,0:T(8,128)(2,1)} %bitcast.43.g_ref), channel_id=1, source_target_pairs={{0,240},{16,224},{32,208},{48,192},{64,176},{80,160},{96,144},{112... | collective-permute-start | bytes 5505032 | tf_op jit(solution)/shard_map/ppermute | solution.py:275
  43.0 19.4 %collective-permute-start.28 = (bf16[192,2048]{1,0:T(8,128)(2,1)}, bf16[192,2048]{1,0:T(8,128)(2,1)}, u32[]{:S(2)}, u32[]{:S(2)}) collective-permute-start(bf16[192,2048]{1,0:T(8,128)(2,1)} %collective-permute-done.27.refs_8_), channel_id=1, source_target_pairs={{0,14},{1,15},{2,0},{3,1},{4,2},{5,3},{6,4},{7,5},{8,6},{9,7},{10,... | collective-permute-start | bytes 2359304 | tf_op jit(solution)/shard_map/ppermute | solution.py:17
  46.8 19.3 %collective-permute-start.25 = (bf16[192,2048]{1,0:T(8,128)(2,1)}, bf16[192,2048]{1,0:T(8,128)(2,1)}, u32[]{:S(2)}, u32[]{:S(2)}) collective-permute-start(bf16[192,2048]{1,0:T(8,128)(2,1)} %collective-permute-done.24.refs_1_), channel_id=1, source_target_pairs={{0,2},{1,3},{2,4},{3,5},{4,6},{5,7},{6,8},{7,9},{8,10},{9,11},{10,... | collective-permute-start | bytes 2359304 | tf_op jit(solution)/shard_map/ppermute | solution.py:17
  62.4 18.4 %collective-permute-start.29 = (bf16[192,2048]{1,0:T(8,128)(2,1)}, bf16[192,2048]{1,0:T(8,128)(2,1)}, u32[]{:S(2)}, u32[]{:S(2)}) collective-permute-start(bf16[192,2048]{1,0:T(8,128)(2,1)} %collective-permute-done.28.refs_7_), channel_id=1, source_target_pairs={{0,14},{1,15},{2,0},{3,1},{4,2},{5,3},{6,4},{7,5},{8,6},{9,7},{10,... | collective-permute-start | bytes 2359304 | tf_op jit(solution)/shard_map/ppermute | solution.py:17
  66.1 19.5 %collective-permute-start.26 = (bf16[192,2048]{1,0:T(8,128)(2,1)}, bf16[192,2048]{1,0:T(8,128)(2,1)}, u32[]{:S(2)}, u32[]{:S(2)}) collective-permute-start(bf16[192,2048]{1,0:T(8,128)(2,1)} %collective-permute-done.25.refs_2_), channel_id=1, source_target_pairs={{0,2},{1,3},{2,4},{3,5},{4,6},{5,7},{6,8},{7,9},{8,10},{9,11},{10,... | collective-permute-start | bytes 2359304 | tf_op jit(solution)/shard_map/ppermute | solution.py:17
  70.3 19.8 %collective-permute-start.1 = (bf16[4,32,512]{2,1,0:T(8,128)(2,1)S(1)}, bf16[4,32,512]{2,1,0:T(8,128)(2,1)S(1)}, u32[]{:S(2)}, u32[]{:S(2)}) collective-permute-start(bf16[4,32,512]{2,1,0:T(8,128)(2,1)S(1)} %get-tuple-element.33), channel_id=1, source_target_pairs={{0,2},{1,3},{2,4},{3,5},{4,6},{5,7},{6,8},{7,9},{8,10},{9,11},{10,... | collective-permute-start | bytes 393224 | tf_op jit(solution)/shard_map/ppermute | solution.py:17
  85.7 117.7 %all-to-all-start.1 = ((bf16[16,128,512]{2,1,0:T(8,128)(2,1)}), bf16[16,128,512]{2,1,0:T(8,128)(2,1)}, u32[]{:S(2)}, u32[]{:S(2)}) async-start(bf16[16,128,512]{2,1,0:T(8,128)(2,1)} %shard_map.86), calls=%async_computation.1 | async-start | bytes 4194304 | tf_op jit(solution)/shard_map/all_to_all | solution.py:332
  90.2 46.9 %collective-permute-start.2 = (bf16[4,32,512]{2,1,0:T(8,128)(2,1)S(1)}, bf16[4,32,512]{2,1,0:T(8,128)(2,1)S(1)}, u32[]{:S(2)}, u32[]{:S(2)}) collective-permute-start(bf16[4,32,512]{2,1,0:T(8,128)(2,1)S(1)} %bitcast_add_fusion.2), channel_id=1, source_target_pairs={{0,2},{1,3},{2,4},{3,5},{4,6},{5,7},{6,8},{7,9},{8,10},{9,11},{10,... | collective-permute-start | bytes 393224 | tf_op jit(solution)/shard_map/ppermute | solution.py:17
  92.3 45.0 %collective-permute-start.5 = (bf16[4,32,512]{2,1,0:T(8,128)(2,1)S(1)}, bf16[4,32,512]{2,1,0:T(8,128)(2,1)S(1)}, u32[]{:S(2)}, u32[]{:S(2)}) collective-permute-start(bf16[4,32,512]{2,1,0:T(8,128)(2,1)S(1)} %get-tuple-element.34), channel_id=1, source_target_pairs={{0,14},{1,15},{2,0},{3,1},{4,2},{5,3},{6,4},{7,5},{8,6},{9,7},{10,... | collective-permute-start | bytes 393224 | tf_op jit(solution)/shard_map/ppermute | solution.py:17
  166.6 96.0 %collective-permute-start.32 = (bf16[192,2048]{1,0:T(8,128)(2,1)}, bf16[192,2048]{1,0:T(8,128)(2,1)}, u32[]{:S(2)}, u32[]{:S(2)}) collective-permute-start(bf16[192,2048]{1,0:T(8,128)(2,1)} %pad_maximum_fusion.2), channel_id=1, source_target_pairs={{0,1},{1,0},{2,3},{3,2},{4,5},{5,4},{6,7},{7,6},{8,9},{9,8},{10,11... | collective-permute-start | bytes 2359304 | tf_op jit(solution)/shard_map/ppermute | solution.py:22
  173.1 23.1 %collective-permute-start.11 = (bf16[432,512]{1,0:T(8,128)(2,1)S(1)}, bf16[432,512]{1,0:T(8,128)(2,1)S(1)}, u32[]{:S(2)}, u32[]{:S(2)}) collective-permute-start(bf16[432,512]{1,0:T(8,128)(2,1)S(1)} %pad_maximum_fusion.5), channel_id=1, source_target_pairs={{0,1},{1,0},{2,3},{3,2},{4,5},{5,4},{6,7},{7,6},{8,9},{9,8},{10,11... | collective-permute-start | bytes 1327112 | tf_op jit(solution)/shard_map/ppermute | solution.py:22
  176.0 32.6 %collective-permute-start.14 = (bf16[288,512]{1,0:T(8,128)(2,1)}, bf16[288,512]{1,0:T(8,128)(2,1)}, u32[]{:S(2)}, u32[]{:S(2)}) collective-permute-start(bf16[288,512]{1,0:T(8,128)(2,1)} %pad_maximum_fusion.6), channel_id=1, source_target_pairs={{0,1},{1,0},{2,3},{3,2},{4,5},{5,4},{6,7},{7,6},{8,9},{9,8},{10,11... | collective-permute-start | bytes 884744 | tf_op jit(solution)/shard_map/ppermute | solution.py:22
  188.0 27.7 %collective-permute-start.17 = (bf16[288,512]{1,0:T(8,128)(2,1)}, bf16[288,512]{1,0:T(8,128)(2,1)}, u32[]{:S(2)}, u32[]{:S(2)}) collective-permute-start(bf16[288,512]{1,0:T(8,128)(2,1)} %pad_maximum_fusion.7), channel_id=1, source_target_pairs={{0,1},{1,0},{2,3},{3,2},{4,5},{5,4},{6,7},{7,6},{8,9},{9,8},{10,11... | collective-permute-start | bytes 884744 | tf_op jit(solution)/shard_map/ppermute | solution.py:22
  196.2 21.4 %collective-permute-start.20 = (bf16[144,512]{1,0:T(8,128)(2,1)}, bf16[144,512]{1,0:T(8,128)(2,1)}, u32[]{:S(2)}, u32[]{:S(2)}) collective-permute-start(bf16[144,512]{1,0:T(8,128)(2,1)} %constant_dynamic-update-slice_fusion), channel_id=1, source_target_pairs={{0,1},{1,0},{2,3},{3,2},{4,5},{5,4},{6,7},{7,6},{8,9},{9,8},{10,11... | collective-permute-start | bytes 442376 | tf_op jit(solution)/shard_map/ppermute | solution.py:22
  203.4 59.3 %all-to-all-start = ((bf16[16,128,512]{2,1,0:T(8,128)(2,1)}), bf16[16,128,512]{2,1,0:T(8,128)(2,1)}, u32[]{:S(2)}, u32[]{:S(2)}) async-start(bf16[16,128,512]{2,1,0:T(8,128)(2,1)} %shard_map.85), calls=%async_computation | async-start | bytes 4194304 | tf_op jit(solution)/shard_map/all_to_all | solution.py:342
  212.4 50.3 %collective-permute-start.33 = (bf16[128,2048]{1,0:T(8,128)(2,1)}, bf16[128,2048]{1,0:T(8,128)(2,1)}, u32[]{:S(2)}, u32[]{:S(2)}) collective-permute-start(bf16[128,2048]{1,0:T(8,128)(2,1)} %pad_maximum_fusion.3), channel_id=1, source_target_pairs={{0,1},{1,0},{2,3},{3,2},{4,5},{5,4},{6,7},{7,6},{8,9},{9,8},{10,11... | collective-permute-start | bytes 1572872 | tf_op jit(solution)/shard_map/ppermute | solution.py:22
  227.8 20.4 %collective-permute-start.31 = (bf16[96,2048]{1,0:T(8,128)(2,1)S(1)}, bf16[96,2048]{1,0:T(8,128)(2,1)S(1)}, u32[]{:S(2)}, u32[]{:S(2)}) collective-permute-start(bf16[96,2048]{1,0:T(8,128)(2,1)S(1)} %slice.125), channel_id=1, source_target_pairs={{0,14},{1,15},{2,0},{3,1},{4,2},{5,3},{6,4},{7,5},{8,6},{9,7},{10,... | collective-permute-start | bytes 1179656 | tf_op jit(solution)/shard_map/ppermute | solution.py:17
  230.5 20.3 %collective-permute-start.30 = (bf16[96,2048]{1,0:T(8,128)(2,1)S(1)}, bf16[96,2048]{1,0:T(8,128)(2,1)}, u32[]{:S(2)}, u32[]{:S(2)}) collective-permute-start(bf16[96,2048]{1,0:T(8,128)(2,1)S(1)} %slice.124), channel_id=1, source_target_pairs={{0,2},{1,3},{2,4},{3,5},{4,6},{5,7},{6,8},{7,9},{8,10},{9,11},{10,... | collective-permute-start | bytes 1179656 | tf_op jit(solution)/shard_map/ppermute | solution.py:17
  234.4 28.3 %collective-permute-start.34 = (bf16[128,2048]{1,0:T(8,128)(2,1)S(1)}, bf16[128,2048]{1,0:T(8,128)(2,1)S(1)}, u32[]{:S(2)}, u32[]{:S(2)}) collective-permute-start(bf16[128,2048]{1,0:T(8,128)(2,1)S(1)} %pad_maximum_fusion.4), channel_id=1, source_target_pairs={{0,1},{1,0},{2,3},{3,2},{4,5},{5,4},{6,7},{7,6},{8,9},{9,8},{10,11... | collective-permute-start | bytes 1572872 | tf_op jit(solution)/shard_map/ppermute | solution.py:22
  248.2 14.4 %collective-permute-start.35 = (bf16[64,2048]{1,0:T(8,128)(2,1)S(1)}, bf16[64,2048]{1,0:T(8,128)(2,1)S(1)}, u32[]{:S(2)}, u32[]{:S(2)}) collective-permute-start(bf16[64,2048]{1,0:T(8,128)(2,1)S(1)} %slice.152), channel_id=1, source_target_pairs={{0,1},{1,0},{2,3},{3,2},{4,5},{5,4},{6,7},{7,6},{8,9},{9,8},{10,11... | collective-permute-start | bytes 786440 | tf_op jit(solution)/shard_map/ppermute | solution.py:22
  (23 other events, 237.4 us)

commit v2 on v1

--- a/solution.py
+++ b/solution.py
@@ -50,10 +50,16 @@
     )
 
 
-def route_kernel(slots_here, pick, limit, g_ref, out_ref):
-    rows, _ = g_ref.shape
-    dests, _, block = out_ref.shape
+def route_kernel(with_pieces, slots_here, pick, limit, count, g_ref, *rest):
+    if with_pieces:
+        inv_ref, out_ref = rest
+    else:
+        (out_ref,) = rest
+    rows, width = g_ref.shape
+    dests = out_ref.shape[0]
+    block = out_ref.shape[2]
     per = rows // MB
+    piece = block // dests
     within = lax.broadcasted_iota(jnp.int32, (per, block), 0)
     keep = [within < limit[m] for m in range(MB)]
 
@@ -66,19 +72,33 @@
                 part = g_ref[pl.ds(m * per, per), pl.ds(start, block)]
                 part = jnp.where(keep[m], part, jnp.zeros_like(part))
                 out_ref[dest, pl.ds(t * rows + m * per, per), :] = part
-
-
-def route(pick, limit, g_rows, dests, slots_here, block):
+            if with_pieces:
+                out_ref[dest, pl.ds(slots_here * rows + t * piece, piece), :] = inv_ref[
+                    t, pl.ds(pl.multiple_of(dest * piece, piece), piece), :
+                ]
+        if not with_pieces:
+            live = jnp.full((16, block), count[0].astype(jnp.float32))
+            out_ref[dest, pl.ds(slots_here * rows, 16), :] = live.astype(out_ref.dtype)
+
+
+def route(pick, limit, count, g_rows, inverses, dests, slots_here, block):
+    rows = slots_here * g_rows.shape[0]
+    operands = [g_rows]
+    if inverses is not None:
+        rows += slots_here * (block // dests)
+        operands.append(inverses)
+    else:
+        rows += 16
     vmem = pl.BlockSpec(memory_space=pltpu.VMEM)
     smem = pl.BlockSpec(memory_space=pltpu.SMEM)
     return pl.pallas_call(
-        functools.partial(route_kernel, slots_here),
-        out_shape=jax.ShapeDtypeStruct((dests, slots_here * g_rows.shape[0], block), jnp.bfloat16),
-        in_specs=[smem, smem, vmem],
+        functools.partial(route_kernel, inverses is not None, slots_here),
+        out_shape=jax.ShapeDtypeStruct((dests, rows, block), jnp.bfloat16),
+        in_specs=[smem, smem, smem] + [vmem] * len(operands),
         out_specs=vmem,
         compiler_params=pltpu.CompilerParams(vmem_limit_bytes=VMEM_BYTES),
         cost_estimate=pl.CostEstimate(flops=0, bytes_accessed=8 * 2**20, transcendentals=0),
-    )(pick, limit, g_rows)
+    )(pick, limit, count, *operands)
 
 
 def pack_routed(rows, source, routed_ref, packed, turned):
@@ -132,8 +152,9 @@
         for ref, start, count in mine[d] + other[d]:
             xs[pl.ds(at, count), :] = ref[pl.ds(start, count), :]
             at += count
-    for t in range(turned.shape[0]):
-        acc_ref[t] = jnp.dot(turned[t], xs[...], preferred_element_type=jnp.float32)
+    both = turned[...].reshape(-1, turned.shape[2])
+    grad = jnp.dot(both, xs[...], preferred_element_type=jnp.float32)
+    acc_ref[...] = grad.reshape(acc_ref.shape)
 
     @pl.when(k == place[2])
     def _():
@@ -175,44 +196,61 @@
     )(source, place, routed, *shards)
 
 
-def last_kernel(rows, first_late, source, place, used, scale, routed_ref, *refs):
-    shards, swapped = refs[:9], refs[9:13]
-    acc_ref, stat1_ref, gram1_ref, inv_ref, a_ref, out_ref, stat_ref, gram_ref, packed, turned, xs = refs[13:]
+def last_kernel(rows, first_late, source, place, used, routed_ref, *refs):
+    shards, swapped = refs[:9], refs[9:14]
+    acc_ref, stat1_ref, gram1_ref, inv_ref, out_ref, stat_ref, gram_ref, packed, turned, xs, a_mat, scale, left_both = refs[14:]
     k = pl.program_id(0)
-    per_token = scale[0]
 
     @pl.when(k == 0)
     def _():
+        total = jnp.zeros(scale.shape, jnp.float32)
+        for n in range(routed_ref.shape[0]):
+            total += routed_ref[n, pl.ds(turned.shape[0] * rows, scale.shape[0]), :].astype(jnp.float32)
+        scale[...] = 1.0 / total
         pack_routed(rows, source, routed_ref, packed, turned)
         for t in range(turned.shape[0]):
             cols = half_columns(packed, t, place[0], stat_ref.shape[2])
             stat = stat1_ref[t] + jnp.dot(turned[t], cols, preferred_element_type=jnp.float32)
-            stat_ref[t] = jnp.where(used[t] > 0, stat * per_token, 0.0).astype(stat_ref.dtype)
-
-    one, two, three, four = swapped
+            stat = stat * scale[:1, : stat.shape[1]]
+            stat_ref[t] = jnp.where(used[t] > 0, stat, 0.0).astype(stat_ref.dtype)
+
+    zero, one, two, three, four = swapped
     late = four.shape[0]
-    partner = [(one, 0), (one, 1), (two, 0), (three, 0), (four, 0), (three, 1), (two, 1), (one, 2)]
+    partner = [(zero, 0), (one, 0), (two, 0), (three, 0), (four, 0), (three, 1), (two, 1), (one, 1)]
     mine = ring_rows(shards, first_late, rows)
+    pieces = ring_rows(shards, first_late + rows, late - rows)
+    piece = a_mat.shape[0] // 16
     at = 0
     for d in range(8):
         ref, number = partner[d]
-        for ref, start, count in mine[d] + [(ref, number * late, rows)]:
-            xs[pl.ds(at, count), :] = ref[pl.ds(start, count), :]
+        for part, start, count in mine[d] + [(ref, number * late, rows)]:
+            xs[pl.ds(at, count), :] = part[pl.ds(start, count), :]
             at += count
-
-    for t in range(turned.shape[0]):
-        grad = acc_ref[t] + jnp.dot(turned[t], xs[...], preferred_element_type=jnp.float32)
-        grad = (grad * per_token).astype(jnp.bfloat16)
-        left = jnp.dot(inv_ref[t], grad, preferred_element_type=jnp.float32).astype(jnp.bfloat16)
-        scaled = jnp.dot(left, a_ref[0], preferred_element_type=jnp.float32)
-        out_ref[t] = jnp.where(used[t] > 0, scaled, 0.0).astype(out_ref.dtype)
+        for n, found in enumerate([pieces[d], [(ref, number * late + rows, piece)]]):
+            to = pl.multiple_of(source[2 * d + n] * piece, piece)
+            for part, start, count in found:
+                a_mat[pl.ds(to, count), :] = part[pl.ds(start, count), :]
+                to += count
+
+    slots_here, block, tokens = turned.shape
+    both = turned[...].reshape(slots_here * block, tokens)
+    grads = jnp.dot(both, xs[...], preferred_element_type=jnp.float32)
+    for t in range(slots_here):
+        grad = acc_ref[t] + grads[t * block : (t + 1) * block]
+        grad = (grad * scale[:1]).astype(jnp.bfloat16)
+        left = jnp.dot(inv_ref[t], grad, preferred_element_type=jnp.float32)
+        left_both[pl.ds(t * block, block), :] = left.astype(jnp.bfloat16)
+    scaled = jnp.dot(left_both[...], a_mat[...], preferred_element_type=jnp.float32)
+    for t in range(slots_here):
+        part = scaled[t * block : (t + 1) * block]
+        out_ref[t] = jnp.where(used[t] > 0, part, 0.0).astype(out_ref.dtype)
 
     @pl.when(k == place[2])
     def _():
-        gram_ref[...] = (gram1_ref[...] + gram_here(place, xs, gram_ref.shape[0])) * per_token
-
-
-def last_part(source, place, used, scale, routed, shards, swapped, acc, stat1, gram1, inverses, a_inverse, rows, first_late):
+        gram_ref[...] = (gram1_ref[...] + gram_here(place, xs, gram_ref.shape[0])) * scale[:1]
+
+
+def last_part(source, place, used, routed, shards, swapped, acc, stat1, gram1, inverses, rows, first_late):
     width = acc.shape[2]
     slots_here, block = inverses.shape[:2]
     tokens = routed.shape[0] * rows
@@ -227,11 +265,10 @@
             jax.ShapeDtypeStruct((slots_here, block, block // 2), jnp.bfloat16),
             jax.ShapeDtypeStruct(gram1.shape, jnp.float32),
         ),
-        in_specs=[smem, smem, smem, smem, vmem]
+        in_specs=[smem, smem, smem, vmem]
         + [column_spec(s, block) for s in list(shards) + list(swapped)]
         + [
             pl.BlockSpec((slots_here, block, block), lambda k: (0, 0, k)), vmem, vmem, vmem,
-            pl.BlockSpec((1, block, block), lambda k: (k, 0, 0)),
         ],
         out_specs=(
             pl.BlockSpec((slots_here, block, block), lambda k: (0, 0, k)),
@@ -242,10 +279,13 @@
             pltpu.VMEM((slots_here, tokens, block), jnp.bfloat16),
             pltpu.VMEM((slots_here, block, tokens), jnp.bfloat16),
             pltpu.VMEM((tokens, block), jnp.bfloat16),
+            pltpu.VMEM((block, block), jnp.bfloat16),
+            pltpu.VMEM((16, block), jnp.float32),
+            pltpu.VMEM((slots_here * block, block), jnp.bfloat16),
         ],
         compiler_params=pltpu.CompilerParams(vmem_limit_bytes=VMEM_BYTES),
         cost_estimate=pl.CostEstimate(flops=flops, bytes_accessed=24 * 2**20, transcendentals=0),
-    )(source, place, used, scale, routed, *shards, *swapped, acc, stat1, gram1, inverses, a_inverse)
+    )(source, place, used, routed, *shards, *swapped, acc, stat1, gram1, inverses)
 
 
 def local(activations, cotangents, mb_count, mb_size, block_slot, inv_blocks):
@@ -269,9 +309,7 @@
     g_raw = cotangents[0, 0]
     local_blocks = inv_blocks[0]
     meta = jnp.concatenate([mb_count[0], mb_size[0, 0]])
-    meta_m = lax.ppermute(meta, "section", mirror)
     x_sent = lax.dynamic_slice_in_dim(x_all, (1 - half) * half_width, half_width, 1)
-    x_m = lax.ppermute(x_sent, "section", mirror)
     g_m = lax.ppermute(g_raw, "section", mirror)
 
     def limits(numbers):
@@ -287,93 +325,62 @@
     my_slots = dp_id * slots_here + jnp.arange(slots_here, dtype=jnp.int32)
     used_here = jnp.any(hidden_table[None, :] == my_slots[:, None], axis=1).astype(jnp.int32)
 
-    z_count = dp_count // 2
-    z_here, x_here = dp_id // 2, lax.rem(dp_id, 2)
-
-    out_own = route(block_pick, limits(meta), g_raw, dp_count, slots_here, block)
-
     live_own = live_mask(meta[0], meta[1:], rows, rows // MB)
+    x_own = lax.dynamic_slice_in_dim(x_all, half * half_width, half_width, 1)
+    x_own = jnp.where(live_own[:, None], x_own, zero_bf)
+    out_own = route(block_pick, limits(meta), jnp.zeros((1,), jnp.int32), g_raw, local_blocks, dp_count, slots_here, block)
+    x_far, out_own, meta_sent, x_sent, g_sent = lax.optimization_barrier((x_swap(x_own), out_own, meta, x_sent, g_raw))
+    meta_m = lax.ppermute(meta_sent, "section", mirror)
+    x_m = lax.ppermute(x_sent, "section", mirror)
+    g_m = lax.ppermute(g_sent, "section", mirror)
     live_mir = live_mask(meta_m[0], meta_m[1:], rows, rows // MB)
     count = jnp.sum(live_own.astype(jnp.int32)) + jnp.sum(live_mir.astype(jnp.int32))
-    x_own = lax.dynamic_slice_in_dim(x_all, half * half_width, half_width, 1)
-    x_own = jnp.where(live_own[:, None], x_own, zero_bf)
     x_mir = jnp.where(live_mir[:, None], x_m, zero_bf)
-    held = rows
-    first_late = 2 * held
-    start = jnp.concatenate([x_own, x_swap(x_own), x_mir], axis=0)
-
-    half_block = block // 2
-    piece = half_block // z_count
-    kept = lax.dynamic_slice_in_dim(local_blocks, x_here * half_block, half_block, 1)
-    given = lax.dynamic_slice_in_dim(local_blocks, (1 - x_here) * half_block, half_block, 1)
-    near = jnp.concatenate([kept, x_swap(given)], axis=0)
-    owner = input_table // slots_here
-    near_index = jnp.where(owner % 2 == x_here, 0, slots_here) + input_table % slots_here
-    part = jnp.where((owner // 2 == z_here)[:, None, None], jnp.take(near, near_index, axis=0), zero_bf)
-    part = part.reshape(input_blocks, z_count, piece, block)
-
-    def part_for(offset):
-        return lax.dynamic_index_in_dim(part, lax.rem(z_here + offset + z_count, z_count), 1, keepdims=False)
-
-    out_mir = route(block_pick, limits(meta_m), g_m, dp_count, slots_here, block)
-
-    def late_swap(*parts):
-        return x_swap(jnp.concatenate([part[first_late:] for part in parts], axis=0))
-
-    up1, down1 = ring_start(start)
-    sum_up, sum_down = z_step(part_for(4), 1), z_step(part_for(-3), -1)
-    one = late_swap(start, up1, down1)
+    own0 = jnp.concatenate([x_own, x_far], axis=0)
+
+    in_own = lax.all_to_all(out_own, "dp", split_axis=0, concat_axis=0, tiled=True)
+    own_up1, own_down1 = ring_start(own0)
+    own_up1, own_down1, in_own, g_m = lax.optimization_barrier((own_up1, own_down1, in_own, g_m))
+
+    piece = block // dp_count
+    pieces = in_own[:, slots_here * rows :].reshape(dp_count * slots_here, piece, block)
+    mine = jnp.take(pieces, input_table, axis=0).transpose(1, 0, 2).reshape(piece, half_width)
+    mir0 = jnp.concatenate([x_mir, mine], axis=0)
+    up1, down1 = ring_start(mir0)
+    zero = x_swap(mir0)
+    own_up2, own_down2 = ring_start_pair(own_up1, own_down1)
+    up1, down1, own_up2, own_down2, zero = lax.optimization_barrier((up1, down1, own_up2, own_down2, zero))
+    one = x_swap(jnp.concatenate([up1, down1], axis=0))
     up2, down2 = ring_start_pair(up1, down1)
-    sum_up, sum_down = z_step(part_for(3) + sum_up, 1), z_step(part_for(-2) + sum_down, -1)
-    two = late_swap(up2, down2)
+    own_up3, own_down3 = ring_start_pair(own_up2, own_down2)
+    out_mir = route(block_pick, limits(meta_m), count.reshape(1), g_m, None, dp_count, slots_here, block)
+    up2, down2, own_up3, own_down3, out_mir = lax.optimization_barrier((up2, down2, own_up3, own_down3, out_mir))
+    two = x_swap(jnp.concatenate([up2, down2], axis=0))
     up3, down3 = ring_start_pair(up2, down2)
-    sum_up, sum_down = z_step(part_for(2) + sum_up, 1), z_step(part_for(-1) + sum_down, -1)
-    up3, down3, out_own = lax.optimization_barrier((up3, down3, out_own))
-    in_own = lax.all_to_all(out_own, "dp", split_axis=0, concat_axis=0, tiled=True)
-    three = late_swap(up3, down3)
+    own_top4, own_bottom4 = ring_end(own_up3, own_down3)
+    up3, down3, own_top4, own_bottom4, one = lax.optimization_barrier((up3, down3, own_top4, own_bottom4, one))
+    three = x_swap(jnp.concatenate([up3, down3], axis=0))
     top4, bottom4 = ring_end(up3, down3)
-    sum_up = z_step(part_for(1) + sum_up, 1)
-    mine = (part_for(0) + sum_up + sum_down).reshape(input_blocks * piece, block)
-    cut = top4.shape[0]
-    opposite = jnp.concatenate([top4, bottom4], axis=0)[first_late:] if first_late < cut else bottom4[first_late - cut :]
-    four = x_swap(opposite)
-    shards = [start, up1, up2, up3, top4, bottom4, down3, down2, down1]
+    top4, bottom4, out_mir, two = lax.optimization_barrier((top4, bottom4, out_mir, two))
+    four = x_swap(jnp.concatenate([top4, bottom4], axis=0))
+    own_shards = [own0, own_up1, own_up2, own_up3, own_top4, own_bottom4, own_down3, own_down2, own_down1]
+    shards = [mir0, up1, up2, up3, top4, bottom4, down3, down2, down1]
 
     in_mir = lax.all_to_all(out_mir, "dp", split_axis=0, concat_axis=0, tiled=True)
 
-    counts = jnp.full((16, block), count.astype(jnp.bfloat16))
-    a0 = jnp.concatenate([mine, counts], axis=0)
-    a_up1, a_down1 = ring_start(a0)
-    a_up2, a_down2 = ring_start_pair(a_up1, a_down1)
-    a_up3, a_down3 = ring_start_pair(a_up2, a_down2)
-    a_four = jnp.concatenate([z_step(a_up3[: a0.shape[0] // 2], 1), z_step(a_down3[a0.shape[0] // 2 :], -1)], axis=0)
-    a_one = x_swap(jnp.concatenate([a0, a_up1, a_down1], axis=0)).reshape(3, -1, block)
-    a_two = x_swap(jnp.concatenate([a_up2, a_down2], axis=0)).reshape(2, -1, block)
-    a_three = x_swap(jnp.concatenate([a_up3, a_down3], axis=0)).reshape(2, -1, block)
-    a_last = x_swap(a_four)
-    near_parts = [a0, a_up1, a_up2, a_up3, a_four, a_down3, a_down2, a_down1]
-    far_parts = [a_one[0], a_one[1], a_two[0], a_three[0], a_last, a_three[1], a_two[1], a_one[2]]
-
-    z_from = lax.rem(z_here - jnp.arange(z_count, dtype=jnp.int32) + z_count, z_count)
+    z_count = dp_count // 2
+    z_from = lax.rem(dp_id // 2 - jnp.arange(z_count, dtype=jnp.int32) + z_count, z_count)
+    x_here = lax.rem(dp_id, 2)
     x_order = jnp.stack([x_here, 1 - x_here])
     source = (z_from[:, None] * 2 + x_order[None, :]).reshape(-1)
     per_block = dp_count // input_blocks
     place = jnp.stack([half, dp_id, dp_id // per_block, lax.rem(dp_id, per_block)]).astype(jnp.int32)
 
-    swapped = [one, two, three, four]
-    in_ring = jnp.stack([p for pair in zip(near_parts, far_parts) for p in pair])
-    token_total = jnp.sum(in_ring[:, input_blocks * piece, 0].astype(jnp.float32)).reshape(1)
-    in_ring = in_ring[:, : input_blocks * piece].reshape(dp_count, input_blocks, piece, block)
-    ordered = (x_order[None, :] * z_count + z_from[:, None]).reshape(-1)
-    matches = ordered[None, :] == jnp.arange(dp_count, dtype=jnp.int32)[:, None]
-    ring_place = jnp.sum(jnp.where(matches, jnp.arange(dp_count, dtype=jnp.int32)[None, :], 0), axis=1)
-    a_inverse = jnp.take(in_ring, ring_place, axis=0).transpose(1, 0, 2, 3).reshape(input_blocks, block, block)
-
-    scale = 1.0 / token_total
-    acc, stat1, gram1 = first_part(source, place, in_own, shards, rows, held, slots_here, block)
+    swapped = [zero, one, two, three, four]
+    acc, stat1, gram1 = first_part(source, place, in_own, own_shards, rows, rows, slots_here, block)
     preconditioned, output_stats, input_stats = last_part(
-        source, place, used_here, scale, in_mir, shards, swapped, acc, stat1, gram1, local_blocks, a_inverse,
-        rows, first_late,
+        source, place, used_here, in_mir, shards, swapped, acc, stat1, gram1, local_blocks,
+        rows, 0,
     )
     return (preconditioned[None], output_stats[None], input_stats[None])
 

time: 283 us -> 266 us (0.940)
  local copies, waits for them, and re-layouts: 25 us -> 8.76 us
  waiting for transfers between devices: 129 us -> 145 us
  starting transfers between devices: 74 us -> 61.2 us
  other arithmetic: 13.3 us -> 9.5 us
    ppermute x23 -> x16, waiting for transfers between devices: 115 us -> 34.8 us  [z_step(): return lax.ppermute(value, 'dp', pairs)]
    ppermute x2, waiting for transfers between devices: 0.16 us -> 67.2 us  [the longest x1 67.2 us: local(): meta_m = lax.ppermute(meta_sent, 'section', mirror)]
    ppermute x10 -> x6, waiting for transfers between devices: 13.8 us -> 28.8 us  [x_swap(): return lax.ppermute(value, 'dp', [(d, d ^ 1) for d in range(count)])]
    all_to_all x1, waiting for transfers between devices: 0.01 us -> 11.6 us  [local(): lax.all_to_all(out_mir, 'dp', split_axis=0, concat_axis=0, tiled=True)]
    ppermute x23 -> x16, starting transfers between devices: 36.2 us -> 26.5 us  [z_step(): return lax.ppermute(value, 'dp', pairs)]
    ppermute x10 -> x6, starting transfers between devices: 25.5 us -> 16.8 us  [x_swap(): return lax.ppermute(value, 'dp', [(d, d ^ 1) for d in range(count)])]
    slice x10 -> x1, local copies, waits for them, and re-layouts: 7.47 us -> 1.18 us  [local(): in_own[:, slots_here * rows:].reshape(dp_count * slots_here, piece, block)]
    all_to_all x1, starting transfers between devices: 4.44 us -> 9.8 us  [local(): lax.all_to_all(out_own, 'dp', split_axis=0, concat_axis=0, tiled=True)]
  transfers between devices with their start and end apart: 38 -> 27, of which waited for: 15 -> 14; matrix products, arithmetic and copies ran while one was open for 13% -> 3% of each run, Pallas kernels for 6% -> 7%
where the time goes in v2:
time: 266 us; the launch traced here: 262 us
  waiting for transfers between devices  145 us (55%)
  starting transfers between devices  61.2 us (23%)
  Pallas kernels  34.3 us (13%)
  other arithmetic  9.5 us (4%)
  local copies, waits for them, and re-layouts  8.76 us (3%)
  between operations  3.03 us (1%)
    ppermute x1, waiting for transfers between devices, local(): meta_m = lax.ppermute(meta_sent, 'section', mirror)  67.2 us
    ppermute x16, waiting for transfers between devices, z_step(): return lax.ppermute(value, 'dp', pairs)  34.8 us
    ppermute x6, waiting for transfers between devices, x_swap(): return lax.ppermute(value, 'dp', [(d, d ^ 1) for d in range(count)])  28.8 us
    ppermute x16, starting transfers between devices, z_step(): return lax.ppermute(value, 'dp', pairs)  26.5 us
    ppermute x6, starting transfers between devices, x_swap(): return lax.ppermute(value, 'dp', [(d, d ^ 1) for d in range(count)])  16.8 us
    pallas_call x1, Pallas kernels, last_part(): pl.pallas_call(functools.partial(last_kernel, rows, first_late), grid=(wi...  15.8 us
    all_to_all x1, waiting for transfers between devices, local(): lax.all_to_all(out_mir, 'dp', split_axis=0, concat_axis=0, tiled=True)  11.6 us
    pallas_call x1, Pallas kernels, first_part(): pl.pallas_call(functools.partial(first_kernel, rows, held), grid=(width /...  11.5 us
  transfers between devices with their start and end apart: 27, of which 14 were waited for; matrix products, arithmetic and copies ran while one was open for 3% of the time, Pallas kernels for 7%

profile of v2, /device:TPU:16, one launch (start us, length us, event | category | flops | bytes accessed | tf_op | source)
XLA Modules:
  0.0 262.0 jit_solution(18406612384644827064)
XLA Ops:
  3.7 3.1 %collective-permute-start = (bf16[64,2048]{1,0:T(8,128)(2,1)S(1)}, bf16[64,2048]{1,0:T(8,128)(2,1)S(1)}, u32[]{:S(2)}, u32[]{:S(2)}) collective-permute-start(bf16[64,2048]{1,0:T(8,128)(2,1)S(1)} %bitcast_select_fusion), channel_id=1, source_target_pairs={{0,1},{1,0},{2,3},{3,2},{4,5},{5,4},{6,7},{7,6},{8,9},{9,8},{10,11... | collective-permute-start | bytes 786440 | tf_op jit(solution)/shard_map/ppermute | solution.py:22
  10.1 3.8 %shard_map.85 = bf16[16,192,512]{2,1,0:T(8,128)(2,1)} custom-call(s32[32]{0:T(128)} %select_reduce_fusion.pick, s32[4]{0:T(128)} %compare_select_fusion.5.limit, s32[1]{0:T(128)} %constant.107.clone.1.count, bf16[64,14336]{1,0:T(8,128)(2,1)} %bitcast.38, bf16[2,512,512]{2,1,0:T(8,128)(2,1)} %bitcast.41), custom_call_target="tpu_custom_call" | custom-call | bytes 8388608 | tf_op jit(solution)/shard_map/pallas_call | solution.py:94
  15.3 9.8 %all-to-all-start = ((bf16[16,192,512]{2,1,0:T(8,128)(2,1)}), bf16[16,192,512]{2,1,0:T(8,128)(2,1)S(1)}, u32[]{:S(2)}, u32[]{:S(2)}) async-start(bf16[16,192,512]{2,1,0:T(8,128)(2,1)} %shard_map.85), calls=%async_computation | async-start | bytes 6291456 | tf_op jit(solution)/shard_map/all_to_all | solution.py:341
  32.4 67.2 %collective-permute-done.1 = s32[5]{0:T(128)S(1)} collective-permute-done((s32[5]{0:T(128)S(1)}, s32[5]{0:T(128)S(1)}, u32[]{:S(2)}, u32[]{:S(2)}) %collective-permute-start.1) | collective-permute-done | bytes 52 | tf_op jit(solution)/shard_map/ppermute | solution.py:333
  101.0 2.9 %collective-permute-done.2 = bf16[64,2048]{1,0:T(8,128)(2,1)S(1)} collective-permute-done((bf16[64,2048]{1,0:T(8,128)(2,1)}, bf16[64,2048]{1,0:T(8,128)(2,1)S(1)}, u32[]{:S(2)}, u32[]{:S(2)}) %collective-permute-start.2) | collective-permute-done | bytes 262176 | tf_op jit(solution)/shard_map/ppermute | solution.py:334
  111.4 3.2 %collective-permute-start.9 = (bf16[128,2048]{1,0:T(8,128)(2,1)}, bf16[128,2048]{1,0:T(8,128)(2,1)}, u32[]{:S(2)}, u32[]{:S(2)}) collective-permute-start(bf16[128,2048]{1,0:T(8,128)(2,1)} %copy-done.18), channel_id=1, source_target_pairs={{0,14},{1,15},{2,0},{3,1},{4,2},{5,3},{6,4},{7,5},{8,6},{9,7},{10,... | collective-permute-start | bytes 1572872 | tf_op jit(solution)/shard_map/ppermute | solution.py:17
  114.7 3.1 %collective-permute-start.10 = (bf16[96,2048]{1,0:T(8,128)(2,1)S(1)}, bf16[96,2048]{1,0:T(8,128)(2,1)S(1)}, u32[]{:S(2)}, u32[]{:S(2)}) collective-permute-start(bf16[96,2048]{1,0:T(8,128)(2,1)S(1)} %pad_maximum_fusion.4.refs_0_), channel_id=1, source_target_pairs={{0,1},{1,0},{2,3},{3,2},{4,5},{5,4},{6,7},{7,6},{8,9},{9,8},{10,11... | collective-permute-start | bytes 1179656 | tf_op jit(solution)/shard_map/ppermute | solution.py:22
  118.0 2.9 %collective-permute-start.7 = (bf16[96,2048]{1,0:T(8,128)(2,1)S(1)}, bf16[96,2048]{1,0:T(8,128)(2,1)S(1)}, u32[]{:S(2)}, u32[]{:S(2)}) collective-permute-start(bf16[96,2048]{1,0:T(8,128)(2,1)S(1)} %pad_maximum_fusion.4.refs_0_), channel_id=1, source_target_pairs={{0,14},{1,15},{2,0},{3,1},{4,2},{5,3},{6,4},{7,5},{8,6},{9,7},{10,... | collective-permute-start | bytes 1179656 | tf_op jit(solution)/shard_map/ppermute | solution.py:17
  121.0 4.5 %collective-permute-done.10.refs_9_ = bf16[96,2048]{1,0:T(8,128)(2,1)S(1)} collective-permute-done((bf16[96,2048]{1,0:T(8,128)(2,1)S(1)}, bf16[96,2048]{1,0:T(8,128)(2,1)S(1)}, u32[]{:S(2)}, u32[]{:S(2)}) %collective-permute-start.10) | collective-permute-done | bytes 393248 | tf_op jit(solution)/shard_map/ppermute | solution.py:22
  125.5 8.3 %collective-permute-done.6.refs_1_ = bf16[96,2048]{1,0:T(8,128)(2,1)S(1)} collective-permute-done((bf16[96,2048]{1,0:T(8,128)(2,1)S(1)}, bf16[96,2048]{1,0:T(8,128)(2,1)S(1)}, u32[]{:S(2)}, u32[]{:S(2)}) %collective-permute-start.6) | collective-permute-done | bytes 393248 | tf_op jit(solution)/shard_map/ppermute | solution.py:17
  137.6 2.9 %collective-permute-start.12 = (bf16[96,2048]{1,0:T(8,128)(2,1)S(1)}, bf16[96,2048]{1,0:T(8,128)(2,1)S(1)}, u32[]{:S(2)}, u32[]{:S(2)}) collective-permute-start(bf16[96,2048]{1,0:T(8,128)(2,1)S(1)} %collective-permute-done.7.refs_8_), channel_id=1, source_target_pairs={{0,14},{1,15},{2,0},{3,1},{4,2},{5,3},{6,4},{7,5},{8,6},{9,7},{10,... | collective-permute-start | bytes 1179656 | tf_op jit(solution)/shard_map/ppermute | solution.py:17
  140.5 3.3 %collective-permute-start.19 = (bf16[192,2048]{1,0:T(8,128)(2,1)S(1)}, bf16[192,2048]{1,0:T(8,128)(2,1)}, u32[]{:S(2)}, u32[]{:S(2)}) collective-permute-start(bf16[192,2048]{1,0:T(8,128)(2,1)S(1)} %pad_maximum_fusion), channel_id=1, source_target_pairs={{0,1},{1,0},{2,3},{3,2},{4,5},{5,4},{6,7},{7,6},{8,9},{9,8},{10,11... | collective-permute-start | bytes 2359304 | tf_op jit(solution)/shard_map/ppermute | solution.py:22
  145.1 3.3 %shard_map.86 = bf16[16,144,512]{2,1,0:T(8,128)(2,1)} custom-call(s32[32]{0:T(128)} %select_reduce_fusion.pick, s32[4]{0:T(128)} %get-tuple-element.75.limit, s32[1]{0:T(128)} %bitcast.20.count, bf16[64,14336]{1,0:T(8,128)(2,1)} %collective-permute-done.5.g_ref), custom_call_target="tpu_custom_call" | custom-call | bytes 8388608 | tf_op jit(solution)/shard_map/pallas_call | solution.py:94
  148.3 7.1 %collective-permute-done.11.refs_2_ = bf16[96,2048]{1,0:T(8,128)(2,1)S(1)} collective-permute-done((bf16[96,2048]{1,0:T(8,128)(2,1)S(1)}, bf16[96,2048]{1,0:T(8,128)(2,1)S(1)}, u32[]{:S(2)}, u32[]{:S(2)}) %collective-permute-start.11) | collective-permute-done | bytes 393248 | tf_op jit(solution)/shard_map/ppermute | solution.py:17
  156.7 3.6 %collective-permute-start.22 = (bf16[192,2048]{1,0:T(8,128)(2,1)S(1)}, bf16[192,2048]{1,0:T(8,128)(2,1)}, u32[]{:S(2)}, u32[]{:S(2)}) collective-permute-start(bf16[192,2048]{1,0:T(8,128)(2,1)S(1)} %pad_maximum_fusion.1), channel_id=1, source_target_pairs={{0,1},{1,0},{2,3},{3,2},{4,5},{5,4},{6,7},{7,6},{8,9},{9,8},{10,11... | collective-permute-start | bytes 2359304 | tf_op jit(solution)/shard_map/ppermute | solution.py:22
  160.3 3.3 %collective-permute-start.15 = (bf16[96,2048]{1,0:T(8,128)(2,1)S(1)}, bf16[96,2048]{1,0:T(8,128)(2,1)S(1)}, u32[]{:S(2)}, u32[]{:S(2)}) collective-permute-start(bf16[96,2048]{1,0:T(8,128)(2,1)S(1)} %collective-permute-done.11.refs_2_), channel_id=1, source_target_pairs={{0,2},{1,3},{2,4},{3,5},{4,6},{5,7},{6,8},{7,9},{8,10},{9,11},{10,... | collective-permute-start | bytes 1179656 | tf_op jit(solution)/shard_map/ppermute | solution.py:17
  167.0 9.1 %collective-permute-done.17.refs_4_ = bf16[64,2048]{1,0:T(8,128)(2,1)S(1)} collective-permute-done((bf16[64,2048]{1,0:T(8,128)(2,1)S(1)}, bf16[64,2048]{1,0:T(8,128)(2,1)S(1)}, u32[]{:S(2)}, u32[]{:S(2)}) %collective-permute-start.17) | collective-permute-done | bytes 262176 | tf_op jit(solution)/shard_map/ppermute | solution.py:17
  181.8 3.5 %collective-permute-done.20.refs_4_ = bf16[48,2048]{1,0:T(8,128)(2,1)S(1)} collective-permute-done((bf16[48,2048]{1,0:T(8,128)(2,1)S(1)}, bf16[48,2048]{1,0:T(8,128)(2,1)S(1)}, u32[]{:S(2)}, u32[]{:S(2)}) %collective-permute-start.20) | collective-permute-done | bytes 196640 | tf_op jit(solution)/shard_map/ppermute | solution.py:17
  186.0 5.3 %all-to-all-start.1 = ((bf16[16,144,512]{2,1,0:T(8,128)(2,1)}), bf16[16,144,512]{2,1,0:T(8,128)(2,1)S(1)}, u32[]{:S(2)}, u32[]{:S(2)}) async-start(bf16[16,144,512]{2,1,0:T(8,128)(2,1)} %shard_map.86), calls=%async_computation.1 | async-start | bytes 4718592 | tf_op jit(solution)/shard_map/all_to_all | solution.py:369
  192.9 3.5 %collective-permute-start.23 = (bf16[192,2048]{1,0:T(8,128)(2,1)S(1)}, bf16[192,2048]{1,0:T(8,128)(2,1)S(1)}, u32[]{:S(2)}, u32[]{:S(2)}) collective-permute-start(bf16[192,2048]{1,0:T(8,128)(2,1)S(1)} %pad_maximum_fusion.2), channel_id=1, source_target_pairs={{0,1},{1,0},{2,3},{3,2},{4,5},{5,4},{6,7},{7,6},{8,9},{9,8},{10,11... | collective-permute-start | bytes 2359304 | tf_op jit(solution)/shard_map/ppermute | solution.py:22
  197.3 11.5 %shard_map.87 = (f32[2,512,2048]{2,1,0:T(8,128)}, f32[2,512,256]{2,1,0:T(8,128)}, f32[128,512]{1,0:T(8,128)}) custom-call(s32[16]{0:T(128)} %add.90.source, s32[4]{0:T(128)} %pad_add_fusion.1.place, bf16[16,192,512]{2,1,0:T(8,128)(2,1)} %copy-done, bf16[128,2048]{1,0:T(8,128)(2,1)} %copy-done.5, bf16[128,2048]{1,0:T(8,128)(2,1)} %copy-done.17, ...), custom_call_target="tpu_custom_call" | custom-call | flops 4831838208 | bytes 16777216 | tf_op jit(solution)/shard_map/pallas_call | solution.py:175
  208.8 24.3 %collective-permute-done.24.refs_13_ = bf16[96,2048]{1,0:T(8,128)(2,1)S(1)} collective-permute-done((bf16[96,2048]{1,0:T(8,128)(2,1)S(1)}, bf16[96,2048]{1,0:T(8,128)(2,1)S(1)}, u32[]{:S(2)}, u32[]{:S(2)}) %collective-permute-start.24) | collective-permute-done | bytes 393248 | tf_op jit(solution)/shard_map/ppermute | solution.py:22
  233.1 11.6 %all-to-all-done.1.routed_ref = bf16[16,144,512]{2,1,0:T(8,128)(2,1)S(1)} async-done(((bf16[16,144,512]{2,1,0:T(8,128)(2,1)}), bf16[16,144,512]{2,1,0:T(8,128)(2,1)S(1)}, u32[]{:S(2)}, u32[]{:S(2)}) %all-to-all-start.1) | async-done | bytes 2359328 | tf_op jit(solution)/shard_map/all_to_all | solution.py:369
  246.1 15.8 %shard_map.88 = (bf16[2,512,2048]{2,1,0:T(8,128)(2,1)}, bf16[2,512,256]{2,1,0:T(8,128)(2,1)}, f32[128,512]{1,0:T(8,128)}) custom-call(s32[16]{0:T(128)} %add.90.source, s32[4]{0:T(128)} %pad_add_fusion.1.place, s32[2]{0:T(128)} %convert_element_type.13.used, bf16[16,144,512]{2,1,0:T(8,128)(2,1)} %copy-done.1, bf16[96,2048]{1,0:T(8,128)(2,1)} %copy-done.6, ...), custom_call_target="tpu_custom_call" | custom-call | flops 8589934592 | bytes 25165824 | tf_op jit(solution)/shard_map/pallas_call | solution.py:260
  (120 shorter events, 42.1 us)
Async XLA Ops:
  3.7 10.9 %collective-permute-start = (bf16[64,2048]{1,0:T(8,128)(2,1)S(1)}, bf16[64,2048]{1,0:T(8,128)(2,1)S(1)}, u32[]{:S(2)}, u32[]{:S(2)}) collective-permute-start(bf16[64,2048]{1,0:T(8,128)(2,1)S(1)} %bitcast_select_fusion), channel_id=1, source_target_pairs={{0,1},{1,0},{2,3},{3,2},{4,5},{5,4},{6,7},{7,6},{8,9},{9,8},{10,11... | collective-permute-start | bytes 786440 | tf_op jit(solution)/shard_map/ppermute | solution.py:22
  15.3 92.7 %all-to-all-start = ((bf16[16,192,512]{2,1,0:T(8,128)(2,1)}), bf16[16,192,512]{2,1,0:T(8,128)(2,1)S(1)}, u32[]{:S(2)}, u32[]{:S(2)}) async-start(bf16[16,192,512]{2,1,0:T(8,128)(2,1)} %shard_map.85), calls=%async_computation | async-start | bytes 6291456 | tf_op jit(solution)/shard_map/all_to_all | solution.py:341
  25.1 82.9 %collective-permute-start.5 = (bf16[64,14336]{1,0:T(8,128)(2,1)}, bf16[64,14336]{1,0:T(8,128)(2,1)}, u32[]{:S(2)}, u32[]{:S(2)}) collective-permute-start(bf16[64,14336]{1,0:T(8,128)(2,1)} %bitcast.39), channel_id=1, source_target_pairs={{0,240},{16,224},{32,208},{48,192},{64,176},{80,160},{96,144},{112... | collective-permute-start | bytes 5505032 | tf_op jit(solution)/shard_map/ppermute | solution.py:335
  26.4 80.0 %collective-permute-start.3 = (bf16[128,2048]{1,0:T(8,128)(2,1)S(1)}, bf16[128,2048]{1,0:T(8,128)(2,1)S(1)}, u32[]{:S(2)}, u32[]{:S(2)}) collective-permute-start(bf16[128,2048]{1,0:T(8,128)(2,1)S(1)} %pad_maximum_fusion.3.refs_0_), channel_id=1, source_target_pairs={{0,2},{1,3},{2,4},{3,5},{4,6},{5,7},{6,8},{7,9},{8,10},{9,11},{10,... | collective-permute-start | bytes 1572872 | tf_op jit(solution)/shard_map/ppermute | solution.py:17
  28.3 78.4 %collective-permute-start.4 = (bf16[128,2048]{1,0:T(8,128)(2,1)S(1)}, bf16[128,2048]{1,0:T(8,128)(2,1)S(1)}, u32[]{:S(2)}, u32[]{:S(2)}) collective-permute-start(bf16[128,2048]{1,0:T(8,128)(2,1)S(1)} %pad_maximum_fusion.3.refs_0_), channel_id=1, source_target_pairs={{0,14},{1,15},{2,0},{3,1},{4,2},{5,3},{6,4},{7,5},{8,6},{9,7},{10,... | collective-permute-start | bytes 1572872 | tf_op jit(solution)/shard_map/ppermute | solution.py:17
  29.7 69.8 %collective-permute-start.1 = (s32[5]{0:T(128)S(1)}, s32[5]{0:T(128)S(1)}, u32[]{:S(2)}, u32[]{:S(2)}) collective-permute-start(s32[5]{0:T(128)S(1)} %pad_add_fusion.2), channel_id=1, source_target_pairs={{0,240},{16,224},{32,208},{48,192},{64,176},{80,160},{96,144},{112... | collective-permute-start | bytes 68 | tf_op jit(solution)/shard_map/ppermute | solution.py:333
  32.0 71.8 %collective-permute-start.2 = (bf16[64,2048]{1,0:T(8,128)(2,1)}, bf16[64,2048]{1,0:T(8,128)(2,1)S(1)}, u32[]{:S(2)}, u32[]{:S(2)}) collective-permute-start(bf16[64,2048]{1,0:T(8,128)(2,1)} %dynamic-slice_bitcast_fusion), channel_id=1, source_target_pairs={{0,240},{16,224},{32,208},{48,192},{64,176},{80,160},{96,144},{112... | collective-permute-start | bytes 786440 | tf_op jit(solution)/shard_map/ppermute | solution.py:334
  111.3 22.5 %collective-permute-start.8 = (bf16[128,2048]{1,0:T(8,128)(2,1)}, bf16[128,2048]{1,0:T(8,128)(2,1)}, u32[]{:S(2)}, u32[]{:S(2)}) collective-permute-start(bf16[128,2048]{1,0:T(8,128)(2,1)} %copy-done.17), channel_id=1, source_target_pairs={{0,2},{1,3},{2,4},{3,5},{4,6},{5,7},{6,8},{7,9},{8,10},{9,11},{10,... | collective-permute-start | bytes 1572872 | tf_op jit(solution)/shard_map/ppermute | solution.py:17
  111.4 22.4 %collective-permute-start.9 = (bf16[128,2048]{1,0:T(8,128)(2,1)}, bf16[128,2048]{1,0:T(8,128)(2,1)}, u32[]{:S(2)}, u32[]{:S(2)}) collective-permute-start(bf16[128,2048]{1,0:T(8,128)(2,1)} %copy-done.18), channel_id=1, source_target_pairs={{0,14},{1,15},{2,0},{3,1},{4,2},{5,3},{6,4},{7,5},{8,6},{9,7},{10,... | collective-permute-start | bytes 1572872 | tf_op jit(solution)/shard_map/ppermute | solution.py:17
  117.7 16.1 %collective-permute-start.6 = (bf16[96,2048]{1,0:T(8,128)(2,1)S(1)}, bf16[96,2048]{1,0:T(8,128)(2,1)S(1)}, u32[]{:S(2)}, u32[]{:S(2)}) collective-permute-start(bf16[96,2048]{1,0:T(8,128)(2,1)S(1)} %pad_maximum_fusion.4.refs_0_), channel_id=1, source_target_pairs={{0,2},{1,3},{2,4},{3,5},{4,6},{5,7},{6,8},{7,9},{8,10},{9,11},{10,... | collective-permute-start | bytes 1179656 | tf_op jit(solution)/shard_map/ppermute | solution.py:17
  118.0 15.8 %collective-permute-start.7 = (bf16[96,2048]{1,0:T(8,128)(2,1)S(1)}, bf16[96,2048]{1,0:T(8,128)(2,1)S(1)}, u32[]{:S(2)}, u32[]{:S(2)}) collective-permute-start(bf16[96,2048]{1,0:T(8,128)(2,1)S(1)} %pad_maximum_fusion.4.refs_0_), channel_id=1, source_target_pairs={{0,14},{1,15},{2,0},{3,1},{4,2},{5,3},{6,4},{7,5},{8,6},{9,7},{10,... | collective-permute-start | bytes 1179656 | tf_op jit(solution)/shard_map/ppermute | solution.py:17
  133.9 22.7 %collective-permute-start.13 = (bf16[128,2048]{1,0:T(8,128)(2,1)}, bf16[128,2048]{1,0:T(8,128)(2,1)S(1)}, u32[]{:S(2)}, u32[]{:S(2)}) collective-permute-start(bf16[128,2048]{1,0:T(8,128)(2,1)} %collective-permute-done.8.refs_2_), channel_id=1, source_target_pairs={{0,2},{1,3},{2,4},{3,5},{4,6},{5,7},{6,8},{7,9},{8,10},{9,11},{10,... | collective-permute-start | bytes 1572872 | tf_op jit(solution)/shard_map/ppermute | solution.py:17
  135.5 21.0 %collective-permute-start.14 = (bf16[128,2048]{1,0:T(8,128)(2,1)}, bf16[128,2048]{1,0:T(8,128)(2,1)S(1)}, u32[]{:S(2)}, u32[]{:S(2)}) collective-permute-start(bf16[128,2048]{1,0:T(8,128)(2,1)} %collective-permute-done.9.refs_7_), channel_id=1, source_target_pairs={{0,14},{1,15},{2,0},{3,1},{4,2},{5,3},{6,4},{7,5},{8,6},{9,7},{10,... | collective-permute-start | bytes 1572872 | tf_op jit(solution)/shard_map/ppermute | solution.py:17
  137.2 18.3 %collective-permute-start.11 = (bf16[96,2048]{1,0:T(8,128)(2,1)S(1)}, bf16[96,2048]{1,0:T(8,128)(2,1)S(1)}, u32[]{:S(2)}, u32[]{:S(2)}) collective-permute-start(bf16[96,2048]{1,0:T(8,128)(2,1)S(1)} %collective-permute-done.6.refs_1_), channel_id=1, source_target_pairs={{0,2},{1,3},{2,4},{3,5},{4,6},{5,7},{6,8},{7,9},{8,10},{9,11},{10,... | collective-permute-start | bytes 1179656 | tf_op jit(solution)/shard_map/ppermute | solution.py:17
  137.6 19.0 %collective-permute-start.12 = (bf16[96,2048]{1,0:T(8,128)(2,1)S(1)}, bf16[96,2048]{1,0:T(8,128)(2,1)S(1)}, u32[]{:S(2)}, u32[]{:S(2)}) collective-permute-start(bf16[96,2048]{1,0:T(8,128)(2,1)S(1)} %collective-permute-done.7.refs_8_), channel_id=1, source_target_pairs={{0,14},{1,15},{2,0},{3,1},{4,2},{5,3},{6,4},{7,5},{8,6},{9,7},{10,... | collective-permute-start | bytes 1179656 | tf_op jit(solution)/shard_map/ppermute | solution.py:17
  140.5 25.2 %collective-permute-start.19 = (bf16[192,2048]{1,0:T(8,128)(2,1)S(1)}, bf16[192,2048]{1,0:T(8,128)(2,1)}, u32[]{:S(2)}, u32[]{:S(2)}) collective-permute-start(bf16[192,2048]{1,0:T(8,128)(2,1)S(1)} %pad_maximum_fusion), channel_id=1, source_target_pairs={{0,1},{1,0},{2,3},{3,2},{4,5},{5,4},{6,7},{7,6},{8,9},{9,8},{10,11... | collective-permute-start | bytes 2359304 | tf_op jit(solution)/shard_map/ppermute | solution.py:22
  156.7 29.3 %collective-permute-start.22 = (bf16[192,2048]{1,0:T(8,128)(2,1)S(1)}, bf16[192,2048]{1,0:T(8,128)(2,1)}, u32[]{:S(2)}, u32[]{:S(2)}) collective-permute-start(bf16[192,2048]{1,0:T(8,128)(2,1)S(1)} %pad_maximum_fusion.1), channel_id=1, source_target_pairs={{0,1},{1,0},{2,3},{3,2},{4,5},{5,4},{6,7},{7,6},{8,9},{9,8},{10,11... | collective-permute-start | bytes 2359304 | tf_op jit(solution)/shard_map/ppermute | solution.py:22
  160.3 18.0 %collective-permute-start.15 = (bf16[96,2048]{1,0:T(8,128)(2,1)S(1)}, bf16[96,2048]{1,0:T(8,128)(2,1)S(1)}, u32[]{:S(2)}, u32[]{:S(2)}) collective-permute-start(bf16[96,2048]{1,0:T(8,128)(2,1)S(1)} %collective-permute-done.11.refs_2_), channel_id=1, source_target_pairs={{0,2},{1,3},{2,4},{3,5},{4,6},{5,7},{6,8},{7,9},{8,10},{9,11},{10,... | collective-permute-start | bytes 1179656 | tf_op jit(solution)/shard_map/ppermute | solution.py:17
  163.5 14.7 %collective-permute-start.16 = (bf16[96,2048]{1,0:T(8,128)(2,1)S(1)}, bf16[96,2048]{1,0:T(8,128)(2,1)S(1)}, u32[]{:S(2)}, u32[]{:S(2)}) collective-permute-start(bf16[96,2048]{1,0:T(8,128)(2,1)S(1)} %collective-permute-done.12.refs_7_), channel_id=1, source_target_pairs={{0,14},{1,15},{2,0},{3,1},{4,2},{5,3},{6,4},{7,5},{8,6},{9,7},{10,... | collective-permute-start | bytes 1179656 | tf_op jit(solution)/shard_map/ppermute | solution.py:17
  163.6 12.6 %collective-permute-start.17 = (bf16[64,2048]{1,0:T(8,128)(2,1)S(1)}, bf16[64,2048]{1,0:T(8,128)(2,1)S(1)}, u32[]{:S(2)}, u32[]{:S(2)}) collective-permute-start(bf16[64,2048]{1,0:T(8,128)(2,1)S(1)} %slice.42), channel_id=1, source_target_pairs={{0,2},{1,3},{2,4},{3,5},{4,6},{5,7},{6,8},{7,9},{8,10},{9,11},{10,... | collective-permute-start | bytes 786440 | tf_op jit(solution)/shard_map/ppermute | solution.py:17
  165.7 12.6 %collective-permute-start.18 = (bf16[64,2048]{1,0:T(8,128)(2,1)S(1)}, bf16[64,2048]{1,0:T(8,128)(2,1)S(1)}, u32[]{:S(2)}, u32[]{:S(2)}) collective-permute-start(bf16[64,2048]{1,0:T(8,128)(2,1)S(1)} %slice.43), channel_id=1, source_target_pairs={{0,14},{1,15},{2,0},{3,1},{4,2},{5,3},{6,4},{7,5},{8,6},{9,7},{10,... | collective-permute-start | bytes 786440 | tf_op jit(solution)/shard_map/ppermute | solution.py:17
  186.0 58.7 %all-to-all-start.1 = ((bf16[16,144,512]{2,1,0:T(8,128)(2,1)}), bf16[16,144,512]{2,1,0:T(8,128)(2,1)S(1)}, u32[]{:S(2)}, u32[]{:S(2)}) async-start(bf16[16,144,512]{2,1,0:T(8,128)(2,1)} %shard_map.86), calls=%async_computation.1 | async-start | bytes 4718592 | tf_op jit(solution)/shard_map/all_to_all | solution.py:369
  192.9 40.2 %collective-permute-start.23 = (bf16[192,2048]{1,0:T(8,128)(2,1)S(1)}, bf16[192,2048]{1,0:T(8,128)(2,1)S(1)}, u32[]{:S(2)}, u32[]{:S(2)}) collective-permute-start(bf16[192,2048]{1,0:T(8,128)(2,1)S(1)} %pad_maximum_fusion.2), channel_id=1, source_target_pairs={{0,1},{1,0},{2,3},{3,2},{4,5},{5,4},{6,7},{7,6},{8,9},{9,8},{10,11... | collective-permute-start | bytes 2359304 | tf_op jit(solution)/shard_map/ppermute | solution.py:22
  197.1 36.0 %collective-permute-start.24 = (bf16[96,2048]{1,0:T(8,128)(2,1)S(1)}, bf16[96,2048]{1,0:T(8,128)(2,1)S(1)}, u32[]{:S(2)}, u32[]{:S(2)}) collective-permute-start(bf16[96,2048]{1,0:T(8,128)(2,1)S(1)} %pad_maximum_fusion.5), channel_id=1, source_target_pairs={{0,1},{1,0},{2,3},{3,2},{4,5},{5,4},{6,7},{7,6},{8,9},{9,8},{10,11... | collective-permute-start | bytes 1179656 | tf_op jit(solution)/shard_map/ppermute | solution.py:22
  (27 other events, 379.0 us)

commit v3 on v2

--- a/solution.py
+++ b/solution.py
@@ -310,7 +310,6 @@
     local_blocks = inv_blocks[0]
     meta = jnp.concatenate([mb_count[0], mb_size[0, 0]])
     x_sent = lax.dynamic_slice_in_dim(x_all, (1 - half) * half_width, half_width, 1)
-    g_m = lax.ppermute(g_raw, "section", mirror)
 
     def limits(numbers):
         return jnp.where(jnp.arange(MB, dtype=jnp.int32) < numbers[0], numbers[1:], 0)
@@ -340,7 +339,6 @@
 
     in_own = lax.all_to_all(out_own, "dp", split_axis=0, concat_axis=0, tiled=True)
     own_up1, own_down1 = ring_start(own0)
-    own_up1, own_down1, in_own, g_m = lax.optimization_barrier((own_up1, own_down1, in_own, g_m))
 
     piece = block // dp_count
     pieces = in_own[:, slots_here * rows :].reshape(dp_count * slots_here, piece, block)
@@ -349,7 +347,7 @@
     up1, down1 = ring_start(mir0)
     zero = x_swap(mir0)
     own_up2, own_down2 = ring_start_pair(own_up1, own_down1)
-    up1, down1, own_up2, own_down2, zero = lax.optimization_barrier((up1, down1, own_up2, own_down2, zero))
+    up1, down1, own_up2, own_down2, zero, g_m = lax.optimization_barrier((up1, down1, own_up2, own_down2, zero, g_m))
     one = x_swap(jnp.concatenate([up1, down1], axis=0))
     up2, down2 = ring_start_pair(up1, down1)
     own_up3, own_down3 = ring_start_pair(own_up2, own_down2)

time: 266 us -> 254 us (0.955); the launches traced: 262 us -> 253 us
  waiting for transfers between devices: 145 us -> 137 us
    ppermute x1, waiting for transfers between devices: 67.2 us -> 1.17 us  [local(): meta_m = lax.ppermute(meta_sent, 'section', mirror)]
    ppermute x16, waiting for transfers between devices: 34.8 us -> 99.3 us  [z_step(): return lax.ppermute(value, 'dp', pairs)]
    all_to_all x1, waiting for transfers between devices: 11.6 us -> 6.77 us  [local(): lax.all_to_all(out_mir, 'dp', split_axis=0, concat_axis=0, tiled=True)]
    ppermute x1, waiting for transfers between devices: 2.85 us -> 0.01 us  [local(): x_m = lax.ppermute(x_sent, 'section', mirror)]
  transfers between devices with their start and end apart: 27 -> 27, of which waited for: 14 -> 14; matrix products, arithmetic and copies ran while one was open for 3% -> 5% of each run, Pallas kernels for 7% -> 7%
where the time goes in v3:
time: 254 us; the launch traced here: 253 us
  waiting for transfers between devices  137 us (54%)
  starting transfers between devices  60.7 us (24%)
  Pallas kernels  34.3 us (14%)
  other arithmetic  9.73 us (4%)
  local copies, waits for them, and re-layouts  8.4 us (3%)
  between operations  2.99 us (1%)
    ppermute x16, waiting for transfers between devices, z_step(): return lax.ppermute(value, 'dp', pairs)  99.3 us
    ppermute x6, waiting for transfers between devices, x_swap(): return lax.ppermute(value, 'dp', [(d, d ^ 1) for d in range(count)])  29.9 us
    ppermute x16, starting transfers between devices, z_step(): return lax.ppermute(value, 'dp', pairs)  26.5 us
    ppermute x6, starting transfers between devices, x_swap(): return lax.ppermute(value, 'dp', [(d, d ^ 1) for d in range(count)])  16.3 us
    pallas_call x1, Pallas kernels, last_part(): pl.pallas_call(functools.partial(last_kernel, rows, first_late), grid=(wi...  15.8 us
    pallas_call x1, Pallas kernels, first_part(): pl.pallas_call(functools.partial(first_kernel, rows, held), grid=(width /...  11.4 us
    all_to_all x1, starting transfers between devices, local(): lax.all_to_all(out_own, 'dp', split_axis=0, concat_axis=0, tiled=True)  9.75 us
    pallas_call x2, Pallas kernels, route(): pl.pallas_call(functools.partial(route_kernel, inverses is not None, slot...  7.1 us
  transfers between devices with their start and end apart: 27, of which 14 were waited for; matrix products, arithmetic and copies ran while one was open for 5% of the time, Pallas kernels for 7%

profile of v3, /device:TPU:16, one launch (start us, length us, event | category | flops | bytes accessed | tf_op | source)
XLA Modules:
  0.0 253.3 jit_solution(15416785884075126361)
XLA Ops:
  3.8 3.1 %collective-permute-start = (bf16[64,2048]{1,0:T(8,128)(2,1)S(1)}, bf16[64,2048]{1,0:T(8,128)(2,1)S(1)}, u32[]{:S(2)}, u32[]{:S(2)}) collective-permute-start(bf16[64,2048]{1,0:T(8,128)(2,1)S(1)} %bitcast_select_fusion), channel_id=1, source_target_pairs={{0,1},{1,0},{2,3},{3,2},{4,5},{5,4},{6,7},{7,6},{8,9},{9,8},{10,11... | collective-permute-start | bytes 786440 | tf_op jit(solution)/shard_map/ppermute | solution.py:22
  10.1 3.8 %shard_map.85 = bf16[16,192,512]{2,1,0:T(8,128)(2,1)} custom-call(s32[32]{0:T(128)} %select_reduce_fusion.pick, s32[4]{0:T(128)} %compare_select_fusion.5.limit, s32[1]{0:T(128)} %constant.107.clone.1.count, bf16[64,14336]{1,0:T(8,128)(2,1)} %bitcast.38, bf16[2,512,512]{2,1,0:T(8,128)(2,1)} %bitcast.41), custom_call_target="tpu_custom_call" | custom-call | bytes 8388608 | tf_op jit(solution)/shard_map/pallas_call | solution.py:94
  15.4 9.8 %all-to-all-start = ((bf16[16,192,512]{2,1,0:T(8,128)(2,1)}), bf16[16,192,512]{2,1,0:T(8,128)(2,1)S(1)}, u32[]{:S(2)}, u32[]{:S(2)}) async-start(bf16[16,192,512]{2,1,0:T(8,128)(2,1)} %shard_map.85), calls=%async_computation | async-start | bytes 6291456 | tf_op jit(solution)/shard_map/all_to_all | solution.py:340
  35.0 71.5 %collective-permute-done.5.refs_1_ = bf16[128,2048]{1,0:T(8,128)(2,1)} collective-permute-done((bf16[128,2048]{1,0:T(8,128)(2,1)S(1)}, bf16[128,2048]{1,0:T(8,128)(2,1)}, u32[]{:S(2)}, u32[]{:S(2)}) %collective-permute-start.5) | collective-permute-done | bytes 524320 | tf_op jit(solution)/shard_map/ppermute | solution.py:17
  106.9 3.1 %collective-permute-start.8 = (bf16[128,2048]{1,0:T(8,128)(2,1)}, bf16[128,2048]{1,0:T(8,128)(2,1)}, u32[]{:S(2)}, u32[]{:S(2)}) collective-permute-start(bf16[128,2048]{1,0:T(8,128)(2,1)} %collective-permute-done.7.refs_8_), channel_id=1, source_target_pairs={{0,14},{1,15},{2,0},{3,1},{4,2},{5,3},{6,4},{7,5},{8,6},{9,7},{10,... | collective-permute-start | bytes 1572872 | tf_op jit(solution)/shard_map/ppermute | solution.py:17
  113.4 3.2 %collective-permute-start.4 = (bf16[96,2048]{1,0:T(8,128)(2,1)S(1)}, bf16[96,2048]{1,0:T(8,128)(2,1)S(1)}, u32[]{:S(2)}, u32[]{:S(2)}) collective-permute-start(bf16[96,2048]{1,0:T(8,128)(2,1)S(1)} %pad_maximum_fusion.4.refs_0_), channel_id=1, source_target_pairs={{0,14},{1,15},{2,0},{3,1},{4,2},{5,3},{6,4},{7,5},{8,6},{9,7},{10,... | collective-permute-start | bytes 1179656 | tf_op jit(solution)/shard_map/ppermute | solution.py:17
  116.6 6.3 %collective-permute-done.6.refs_2_ = bf16[128,2048]{1,0:T(8,128)(2,1)} collective-permute-done((bf16[128,2048]{1,0:T(8,128)(2,1)}, bf16[128,2048]{1,0:T(8,128)(2,1)}, u32[]{:S(2)}, u32[]{:S(2)}) %collective-permute-start.6) | collective-permute-done | bytes 524320 | tf_op jit(solution)/shard_map/ppermute | solution.py:17
  125.9 3.1 %collective-permute-done.3.refs_1_ = bf16[96,2048]{1,0:T(8,128)(2,1)S(1)} collective-permute-done((bf16[96,2048]{1,0:T(8,128)(2,1)S(1)}, bf16[96,2048]{1,0:T(8,128)(2,1)S(1)}, u32[]{:S(2)}, u32[]{:S(2)}) %collective-permute-start.3) | collective-permute-done | bytes 393248 | tf_op jit(solution)/shard_map/ppermute | solution.py:17
  128.9 3.2 %collective-permute-done.9.refs_9_ = bf16[96,2048]{1,0:T(8,128)(2,1)S(1)} collective-permute-done((bf16[96,2048]{1,0:T(8,128)(2,1)S(1)}, bf16[96,2048]{1,0:T(8,128)(2,1)S(1)}, u32[]{:S(2)}, u32[]{:S(2)}) %collective-permute-start.9) | collective-permute-done | bytes 393248 | tf_op jit(solution)/shard_map/ppermute | solution.py:22
  132.2 3.2 %collective-permute-start.14 = (bf16[128,2048]{1,0:T(8,128)(2,1)}, bf16[128,2048]{1,0:T(8,128)(2,1)}, u32[]{:S(2)}, u32[]{:S(2)}) collective-permute-start(bf16[128,2048]{1,0:T(8,128)(2,1)} %collective-permute-done.8.refs_7_), channel_id=1, source_target_pairs={{0,14},{1,15},{2,0},{3,1},{4,2},{5,3},{6,4},{7,5},{8,6},{9,7},{10,... | collective-permute-start | bytes 1572872 | tf_op jit(solution)/shard_map/ppermute | solution.py:17
  135.4 3.2 %collective-permute-start.12 = (bf16[96,2048]{1,0:T(8,128)(2,1)S(1)}, bf16[96,2048]{1,0:T(8,128)(2,1)S(1)}, u32[]{:S(2)}, u32[]{:S(2)}) collective-permute-start(bf16[96,2048]{1,0:T(8,128)(2,1)S(1)} %collective-permute-done.4.refs_8_), channel_id=1, source_target_pairs={{0,14},{1,15},{2,0},{3,1},{4,2},{5,3},{6,4},{7,5},{8,6},{9,7},{10,... | collective-permute-start | bytes 1179656 | tf_op jit(solution)/shard_map/ppermute | solution.py:17
  138.7 3.1 %collective-permute-start.19 = (bf16[192,2048]{1,0:T(8,128)(2,1)S(1)}, bf16[192,2048]{1,0:T(8,128)(2,1)}, u32[]{:S(2)}, u32[]{:S(2)}) collective-permute-start(bf16[192,2048]{1,0:T(8,128)(2,1)S(1)} %pad_maximum_fusion), channel_id=1, source_target_pairs={{0,1},{1,0},{2,3},{3,2},{4,5},{5,4},{6,7},{7,6},{8,9},{9,8},{10,11... | collective-permute-start | bytes 2359304 | tf_op jit(solution)/shard_map/ppermute | solution.py:22
  143.0 3.3 %shard_map.86 = bf16[16,144,512]{2,1,0:T(8,128)(2,1)} custom-call(s32[32]{0:T(128)} %select_reduce_fusion.pick, s32[4]{0:T(128)} %get-tuple-element.69.limit, s32[1]{0:T(128)} %bitcast.20.count, bf16[64,14336]{1,0:T(8,128)(2,1)} %collective-permute-done.10.g_ref), custom_call_target="tpu_custom_call" | custom-call | bytes 8388608 | tf_op jit(solution)/shard_map/pallas_call | solution.py:94
  146.3 4.2 %collective-permute-done.11.refs_2_ = bf16[96,2048]{1,0:T(8,128)(2,1)S(1)} collective-permute-done((bf16[96,2048]{1,0:T(8,128)(2,1)S(1)}, bf16[96,2048]{1,0:T(8,128)(2,1)S(1)}, u32[]{:S(2)}, u32[]{:S(2)}) %collective-permute-start.11) | collective-permute-done | bytes 393248 | tf_op jit(solution)/shard_map/ppermute | solution.py:17
  150.8 3.5 %collective-permute-start.22 = (bf16[192,2048]{1,0:T(8,128)(2,1)S(1)}, bf16[192,2048]{1,0:T(8,128)(2,1)}, u32[]{:S(2)}, u32[]{:S(2)}) collective-permute-start(bf16[192,2048]{1,0:T(8,128)(2,1)S(1)} %pad_maximum_fusion.1), channel_id=1, source_target_pairs={{0,1},{1,0},{2,3},{3,2},{4,5},{5,4},{6,7},{7,6},{8,9},{9,8},{10,11... | collective-permute-start | bytes 2359304 | tf_op jit(solution)/shard_map/ppermute | solution.py:22
  154.3 3.6 %collective-permute-start.15 = (bf16[96,2048]{1,0:T(8,128)(2,1)S(1)}, bf16[96,2048]{1,0:T(8,128)(2,1)S(1)}, u32[]{:S(2)}, u32[]{:S(2)}) collective-permute-start(bf16[96,2048]{1,0:T(8,128)(2,1)S(1)} %collective-permute-done.11.refs_2_), channel_id=1, source_target_pairs={{0,2},{1,3},{2,4},{3,5},{4,6},{5,7},{6,8},{7,9},{8,10},{9,11},{10,... | collective-permute-start | bytes 1179656 | tf_op jit(solution)/shard_map/ppermute | solution.py:17
  162.3 7.8 %collective-permute-done.17.refs_4_ = bf16[64,2048]{1,0:T(8,128)(2,1)S(1)} collective-permute-done((bf16[64,2048]{1,0:T(8,128)(2,1)S(1)}, bf16[64,2048]{1,0:T(8,128)(2,1)S(1)}, u32[]{:S(2)}, u32[]{:S(2)}) %collective-permute-start.17) | collective-permute-done | bytes 262176 | tf_op jit(solution)/shard_map/ppermute | solution.py:17
  175.6 3.5 %collective-permute-done.20.refs_4_ = bf16[48,2048]{1,0:T(8,128)(2,1)S(1)} collective-permute-done((bf16[48,2048]{1,0:T(8,128)(2,1)S(1)}, bf16[48,2048]{1,0:T(8,128)(2,1)S(1)}, u32[]{:S(2)}, u32[]{:S(2)}) %collective-permute-start.20) | collective-permute-done | bytes 196640 | tf_op jit(solution)/shard_map/ppermute | solution.py:17
  179.6 5.4 %all-to-all-start.1 = ((bf16[16,144,512]{2,1,0:T(8,128)(2,1)}), bf16[16,144,512]{2,1,0:T(8,128)(2,1)S(1)}, u32[]{:S(2)}, u32[]{:S(2)}) async-start(bf16[16,144,512]{2,1,0:T(8,128)(2,1)} %shard_map.86), calls=%async_computation.1 | async-start | bytes 4718592 | tf_op jit(solution)/shard_map/all_to_all | solution.py:367
  186.6 3.5 %collective-permute-start.23 = (bf16[192,2048]{1,0:T(8,128)(2,1)S(1)}, bf16[192,2048]{1,0:T(8,128)(2,1)S(1)}, u32[]{:S(2)}, u32[]{:S(2)}) collective-permute-start(bf16[192,2048]{1,0:T(8,128)(2,1)S(1)} %pad_maximum_fusion.2), channel_id=1, source_target_pairs={{0,1},{1,0},{2,3},{3,2},{4,5},{5,4},{6,7},{7,6},{8,9},{9,8},{10,11... | collective-permute-start | bytes 2359304 | tf_op jit(solution)/shard_map/ppermute | solution.py:22
  191.0 11.4 %shard_map.87 = (f32[2,512,2048]{2,1,0:T(8,128)}, f32[2,512,256]{2,1,0:T(8,128)}, f32[128,512]{1,0:T(8,128)}) custom-call(s32[16]{0:T(128)} %add.90.source, s32[4]{0:T(128)} %pad_add_fusion.1.place, bf16[16,192,512]{2,1,0:T(8,128)(2,1)} %copy-done, bf16[128,2048]{1,0:T(8,128)(2,1)} %copy-done.5, bf16[128,2048]{1,0:T(8,128)(2,1)} %collective-permute-done.5.refs_1_, ...), custom_call_target="tpu_custom_call" | custom-call | flops 4831838208 | bytes 16777216 | tf_op jit(solution)/shard_map/pallas_call | solution.py:175
  202.5 26.7 %collective-permute-done.24.refs_13_ = bf16[96,2048]{1,0:T(8,128)(2,1)S(1)} collective-permute-done((bf16[96,2048]{1,0:T(8,128)(2,1)S(1)}, bf16[96,2048]{1,0:T(8,128)(2,1)S(1)}, u32[]{:S(2)}, u32[]{:S(2)}) %collective-permute-start.24) | collective-permute-done | bytes 393248 | tf_op jit(solution)/shard_map/ppermute | solution.py:22
  229.1 6.8 %all-to-all-done.1.routed_ref = bf16[16,144,512]{2,1,0:T(8,128)(2,1)S(1)} async-done(((bf16[16,144,512]{2,1,0:T(8,128)(2,1)}), bf16[16,144,512]{2,1,0:T(8,128)(2,1)S(1)}, u32[]{:S(2)}, u32[]{:S(2)}) %all-to-all-start.1) | async-done | bytes 2359328 | tf_op jit(solution)/shard_map/all_to_all | solution.py:367
  237.4 15.8 %shard_map.88 = (bf16[2,512,2048]{2,1,0:T(8,128)(2,1)}, bf16[2,512,256]{2,1,0:T(8,128)(2,1)}, f32[128,512]{1,0:T(8,128)}) custom-call(s32[16]{0:T(128)} %add.90.source, s32[4]{0:T(128)} %pad_add_fusion.1.place, s32[2]{0:T(128)} %convert_element_type.13.used, bf16[16,144,512]{2,1,0:T(8,128)(2,1)} %copy-done.1, bf16[96,2048]{1,0:T(8,128)(2,1)} %copy-done.6, ...), custom_call_target="tpu_custom_call" | custom-call | flops 8589934592 | bytes 25165824 | tf_op jit(solution)/shard_map/pallas_call | solution.py:260
  (114 shorter events, 38.3 us)
Async XLA Ops:
  3.8 10.9 %collective-permute-start = (bf16[64,2048]{1,0:T(8,128)(2,1)S(1)}, bf16[64,2048]{1,0:T(8,128)(2,1)S(1)}, u32[]{:S(2)}, u32[]{:S(2)}) collective-permute-start(bf16[64,2048]{1,0:T(8,128)(2,1)S(1)} %bitcast_select_fusion), channel_id=1, source_target_pairs={{0,1},{1,0},{2,3},{3,2},{4,5},{5,4},{6,7},{7,6},{8,9},{9,8},{10,11... | collective-permute-start | bytes 786440 | tf_op jit(solution)/shard_map/ppermute | solution.py:22
  15.4 94.5 %all-to-all-start = ((bf16[16,192,512]{2,1,0:T(8,128)(2,1)}), bf16[16,192,512]{2,1,0:T(8,128)(2,1)S(1)}, u32[]{:S(2)}, u32[]{:S(2)}) async-start(bf16[16,192,512]{2,1,0:T(8,128)(2,1)} %shard_map.85), calls=%async_computation | async-start | bytes 6291456 | tf_op jit(solution)/shard_map/all_to_all | solution.py:340
  26.3 80.2 %collective-permute-start.5 = (bf16[128,2048]{1,0:T(8,128)(2,1)S(1)}, bf16[128,2048]{1,0:T(8,128)(2,1)}, u32[]{:S(2)}, u32[]{:S(2)}) collective-permute-start(bf16[128,2048]{1,0:T(8,128)(2,1)S(1)} %pad_maximum_fusion.3.refs_0_), channel_id=1, source_target_pairs={{0,2},{1,3},{2,4},{3,5},{4,6},{5,7},{6,8},{7,9},{8,10},{9,11},{10,... | collective-permute-start | bytes 1572872 | tf_op jit(solution)/shard_map/ppermute | solution.py:17
  28.3 78.5 %collective-permute-start.7 = (bf16[128,2048]{1,0:T(8,128)(2,1)S(1)}, bf16[128,2048]{1,0:T(8,128)(2,1)}, u32[]{:S(2)}, u32[]{:S(2)}) collective-permute-start(bf16[128,2048]{1,0:T(8,128)(2,1)S(1)} %pad_maximum_fusion.3.refs_0_), channel_id=1, source_target_pairs={{0,14},{1,15},{2,0},{3,1},{4,2},{5,3},{6,4},{7,5},{8,6},{9,7},{10,... | collective-permute-start | bytes 1572872 | tf_op jit(solution)/shard_map/ppermute | solution.py:17
  29.6 76.9 %collective-permute-start.2 = (bf16[64,2048]{1,0:T(8,128)(2,1)}, bf16[64,2048]{1,0:T(8,128)(2,1)S(1)}, u32[]{:S(2)}, u32[]{:S(2)}) collective-permute-start(bf16[64,2048]{1,0:T(8,128)(2,1)} %dynamic-slice_bitcast_fusion), channel_id=1, source_target_pairs={{0,240},{16,224},{32,208},{48,192},{64,176},{80,160},{96,144},{112... | collective-permute-start | bytes 786440 | tf_op jit(solution)/shard_map/ppermute | solution.py:333
  32.3 93.6 %collective-permute-start.10 = (bf16[64,14336]{1,0:T(8,128)(2,1)}, bf16[64,14336]{1,0:T(8,128)(2,1)}, u32[]{:S(2)}, u32[]{:S(2)}) collective-permute-start(bf16[64,14336]{1,0:T(8,128)(2,1)} %bitcast.39), channel_id=1, source_target_pairs={{0,240},{16,224},{32,208},{48,192},{64,176},{80,160},{96,144},{112... | collective-permute-start | bytes 5505032 | tf_op jit(solution)/shard_map/ppermute | solution.py:334
  106.5 16.4 %collective-permute-start.6 = (bf16[128,2048]{1,0:T(8,128)(2,1)}, bf16[128,2048]{1,0:T(8,128)(2,1)}, u32[]{:S(2)}, u32[]{:S(2)}) collective-permute-start(bf16[128,2048]{1,0:T(8,128)(2,1)} %collective-permute-done.5.refs_1_), channel_id=1, source_target_pairs={{0,2},{1,3},{2,4},{3,5},{4,6},{5,7},{6,8},{7,9},{8,10},{9,11},{10,... | collective-permute-start | bytes 1572872 | tf_op jit(solution)/shard_map/ppermute | solution.py:17
  106.9 19.0 %collective-permute-start.8 = (bf16[128,2048]{1,0:T(8,128)(2,1)}, bf16[128,2048]{1,0:T(8,128)(2,1)}, u32[]{:S(2)}, u32[]{:S(2)}) collective-permute-start(bf16[128,2048]{1,0:T(8,128)(2,1)} %collective-permute-done.7.refs_8_), channel_id=1, source_target_pairs={{0,14},{1,15},{2,0},{3,1},{4,2},{5,3},{6,4},{7,5},{8,6},{9,7},{10,... | collective-permute-start | bytes 1572872 | tf_op jit(solution)/shard_map/ppermute | solution.py:17
  113.3 15.6 %collective-permute-start.3 = (bf16[96,2048]{1,0:T(8,128)(2,1)S(1)}, bf16[96,2048]{1,0:T(8,128)(2,1)S(1)}, u32[]{:S(2)}, u32[]{:S(2)}) collective-permute-start(bf16[96,2048]{1,0:T(8,128)(2,1)S(1)} %pad_maximum_fusion.4.refs_0_), channel_id=1, source_target_pairs={{0,2},{1,3},{2,4},{3,5},{4,6},{5,7},{6,8},{7,9},{8,10},{9,11},{10,... | collective-permute-start | bytes 1179656 | tf_op jit(solution)/shard_map/ppermute | solution.py:17
  113.4 15.5 %collective-permute-start.4 = (bf16[96,2048]{1,0:T(8,128)(2,1)S(1)}, bf16[96,2048]{1,0:T(8,128)(2,1)S(1)}, u32[]{:S(2)}, u32[]{:S(2)}) collective-permute-start(bf16[96,2048]{1,0:T(8,128)(2,1)S(1)} %pad_maximum_fusion.4.refs_0_), channel_id=1, source_target_pairs={{0,14},{1,15},{2,0},{3,1},{4,2},{5,3},{6,4},{7,5},{8,6},{9,7},{10,... | collective-permute-start | bytes 1179656 | tf_op jit(solution)/shard_map/ppermute | solution.py:17
  122.9 9.3 %collective-permute-start.9 = (bf16[96,2048]{1,0:T(8,128)(2,1)S(1)}, bf16[96,2048]{1,0:T(8,128)(2,1)S(1)}, u32[]{:S(2)}, u32[]{:S(2)}) collective-permute-start(bf16[96,2048]{1,0:T(8,128)(2,1)S(1)} %pad_maximum_fusion.4.refs_0_), channel_id=1, source_target_pairs={{0,1},{1,0},{2,3},{3,2},{4,5},{5,4},{6,7},{7,6},{8,9},{9,8},{10,11... | collective-permute-start | bytes 1179656 | tf_op jit(solution)/shard_map/ppermute | solution.py:22
  132.2 18.6 %collective-permute-start.13 = (bf16[128,2048]{1,0:T(8,128)(2,1)}, bf16[128,2048]{1,0:T(8,128)(2,1)S(1)}, u32[]{:S(2)}, u32[]{:S(2)}) collective-permute-start(bf16[128,2048]{1,0:T(8,128)(2,1)} %collective-permute-done.6.refs_2_), channel_id=1, source_target_pairs={{0,2},{1,3},{2,4},{3,5},{4,6},{5,7},{6,8},{7,9},{8,10},{9,11},{10,... | collective-permute-start | bytes 1572872 | tf_op jit(solution)/shard_map/ppermute | solution.py:17
  132.2 18.6 %collective-permute-start.14 = (bf16[128,2048]{1,0:T(8,128)(2,1)}, bf16[128,2048]{1,0:T(8,128)(2,1)}, u32[]{:S(2)}, u32[]{:S(2)}) collective-permute-start(bf16[128,2048]{1,0:T(8,128)(2,1)} %collective-permute-done.8.refs_7_), channel_id=1, source_target_pairs={{0,14},{1,15},{2,0},{3,1},{4,2},{5,3},{6,4},{7,5},{8,6},{9,7},{10,... | collective-permute-start | bytes 1572872 | tf_op jit(solution)/shard_map/ppermute | solution.py:17
  135.4 15.1 %collective-permute-start.11 = (bf16[96,2048]{1,0:T(8,128)(2,1)S(1)}, bf16[96,2048]{1,0:T(8,128)(2,1)S(1)}, u32[]{:S(2)}, u32[]{:S(2)}) collective-permute-start(bf16[96,2048]{1,0:T(8,128)(2,1)S(1)} %collective-permute-done.3.refs_1_), channel_id=1, source_target_pairs={{0,2},{1,3},{2,4},{3,5},{4,6},{5,7},{6,8},{7,9},{8,10},{9,11},{10,... | collective-permute-start | bytes 1179656 | tf_op jit(solution)/shard_map/ppermute | solution.py:17
  135.4 15.3 %collective-permute-start.12 = (bf16[96,2048]{1,0:T(8,128)(2,1)S(1)}, bf16[96,2048]{1,0:T(8,128)(2,1)S(1)}, u32[]{:S(2)}, u32[]{:S(2)}) collective-permute-start(bf16[96,2048]{1,0:T(8,128)(2,1)S(1)} %collective-permute-done.4.refs_8_), channel_id=1, source_target_pairs={{0,14},{1,15},{2,0},{3,1},{4,2},{5,3},{6,4},{7,5},{8,6},{9,7},{10,... | collective-permute-start | bytes 1179656 | tf_op jit(solution)/shard_map/ppermute | solution.py:17
  138.7 22.2 %collective-permute-start.19 = (bf16[192,2048]{1,0:T(8,128)(2,1)S(1)}, bf16[192,2048]{1,0:T(8,128)(2,1)}, u32[]{:S(2)}, u32[]{:S(2)}) collective-permute-start(bf16[192,2048]{1,0:T(8,128)(2,1)S(1)} %pad_maximum_fusion), channel_id=1, source_target_pairs={{0,1},{1,0},{2,3},{3,2},{4,5},{5,4},{6,7},{7,6},{8,9},{9,8},{10,11... | collective-permute-start | bytes 2359304 | tf_op jit(solution)/shard_map/ppermute | solution.py:22
  150.8 28.7 %collective-permute-start.22 = (bf16[192,2048]{1,0:T(8,128)(2,1)S(1)}, bf16[192,2048]{1,0:T(8,128)(2,1)}, u32[]{:S(2)}, u32[]{:S(2)}) collective-permute-start(bf16[192,2048]{1,0:T(8,128)(2,1)S(1)} %pad_maximum_fusion.1), channel_id=1, source_target_pairs={{0,1},{1,0},{2,3},{3,2},{4,5},{5,4},{6,7},{7,6},{8,9},{9,8},{10,11... | collective-permute-start | bytes 2359304 | tf_op jit(solution)/shard_map/ppermute | solution.py:22
  154.3 17.8 %collective-permute-start.15 = (bf16[96,2048]{1,0:T(8,128)(2,1)S(1)}, bf16[96,2048]{1,0:T(8,128)(2,1)S(1)}, u32[]{:S(2)}, u32[]{:S(2)}) collective-permute-start(bf16[96,2048]{1,0:T(8,128)(2,1)S(1)} %collective-permute-done.11.refs_2_), channel_id=1, source_target_pairs={{0,2},{1,3},{2,4},{3,5},{4,6},{5,7},{6,8},{7,9},{8,10},{9,11},{10,... | collective-permute-start | bytes 1179656 | tf_op jit(solution)/shard_map/ppermute | solution.py:17
  157.9 14.3 %collective-permute-start.16 = (bf16[96,2048]{1,0:T(8,128)(2,1)S(1)}, bf16[96,2048]{1,0:T(8,128)(2,1)S(1)}, u32[]{:S(2)}, u32[]{:S(2)}) collective-permute-start(bf16[96,2048]{1,0:T(8,128)(2,1)S(1)} %collective-permute-done.12.refs_7_), channel_id=1, source_target_pairs={{0,14},{1,15},{2,0},{3,1},{4,2},{5,3},{6,4},{7,5},{8,6},{9,7},{10,... | collective-permute-start | bytes 1179656 | tf_op jit(solution)/shard_map/ppermute | solution.py:17
  157.9 12.1 %collective-permute-start.17 = (bf16[64,2048]{1,0:T(8,128)(2,1)S(1)}, bf16[64,2048]{1,0:T(8,128)(2,1)S(1)}, u32[]{:S(2)}, u32[]{:S(2)}) collective-permute-start(bf16[64,2048]{1,0:T(8,128)(2,1)S(1)} %slice.42), channel_id=1, source_target_pairs={{0,2},{1,3},{2,4},{3,5},{4,6},{5,7},{6,8},{7,9},{8,10},{9,11},{10,... | collective-permute-start | bytes 786440 | tf_op jit(solution)/shard_map/ppermute | solution.py:17
  161.0 11.1 %collective-permute-start.18 = (bf16[64,2048]{1,0:T(8,128)(2,1)S(1)}, bf16[64,2048]{1,0:T(8,128)(2,1)S(1)}, u32[]{:S(2)}, u32[]{:S(2)}) collective-permute-start(bf16[64,2048]{1,0:T(8,128)(2,1)S(1)} %slice.43), channel_id=1, source_target_pairs={{0,14},{1,15},{2,0},{3,1},{4,2},{5,3},{6,4},{7,5},{8,6},{9,7},{10,... | collective-permute-start | bytes 786440 | tf_op jit(solution)/shard_map/ppermute | solution.py:17
  179.6 56.4 %all-to-all-start.1 = ((bf16[16,144,512]{2,1,0:T(8,128)(2,1)}), bf16[16,144,512]{2,1,0:T(8,128)(2,1)S(1)}, u32[]{:S(2)}, u32[]{:S(2)}) async-start(bf16[16,144,512]{2,1,0:T(8,128)(2,1)} %shard_map.86), calls=%async_computation.1 | async-start | bytes 4718592 | tf_op jit(solution)/shard_map/all_to_all | solution.py:367
  186.6 42.5 %collective-permute-start.23 = (bf16[192,2048]{1,0:T(8,128)(2,1)S(1)}, bf16[192,2048]{1,0:T(8,128)(2,1)S(1)}, u32[]{:S(2)}, u32[]{:S(2)}) collective-permute-start(bf16[192,2048]{1,0:T(8,128)(2,1)S(1)} %pad_maximum_fusion.2), channel_id=1, source_target_pairs={{0,1},{1,0},{2,3},{3,2},{4,5},{5,4},{6,7},{7,6},{8,9},{9,8},{10,11... | collective-permute-start | bytes 2359304 | tf_op jit(solution)/shard_map/ppermute | solution.py:22
  190.8 38.3 %collective-permute-start.24 = (bf16[96,2048]{1,0:T(8,128)(2,1)S(1)}, bf16[96,2048]{1,0:T(8,128)(2,1)S(1)}, u32[]{:S(2)}, u32[]{:S(2)}) collective-permute-start(bf16[96,2048]{1,0:T(8,128)(2,1)S(1)} %pad_maximum_fusion.5), channel_id=1, source_target_pairs={{0,1},{1,0},{2,3},{3,2},{4,5},{5,4},{6,7},{7,6},{8,9},{9,8},{10,11... | collective-permute-start | bytes 1179656 | tf_op jit(solution)/shard_map/ppermute | solution.py:22
  (24 other events, 339.5 us)

commit v4 on v3

--- a/solution.py
+++ b/solution.py
@@ -347,12 +347,12 @@
     up1, down1 = ring_start(mir0)
     zero = x_swap(mir0)
     own_up2, own_down2 = ring_start_pair(own_up1, own_down1)
-    up1, down1, own_up2, own_down2, zero, g_m = lax.optimization_barrier((up1, down1, own_up2, own_down2, zero, g_m))
+    up1, down1, own_up2, own_down2, g_m = lax.optimization_barrier((up1, down1, own_up2, own_down2, g_m))
     one = x_swap(jnp.concatenate([up1, down1], axis=0))
     up2, down2 = ring_start_pair(up1, down1)
     own_up3, own_down3 = ring_start_pair(own_up2, own_down2)
     out_mir = route(block_pick, limits(meta_m), count.reshape(1), g_m, None, dp_count, slots_here, block)
-    up2, down2, own_up3, own_down3, out_mir = lax.optimization_barrier((up2, down2, own_up3, own_down3, out_mir))
+    up2, down2, own_up3, own_down3, out_mir, zero = lax.optimization_barrier((up2, down2, own_up3, own_down3, out_mir, zero))
     two = x_swap(jnp.concatenate([up2, down2], axis=0))
     up3, down3 = ring_start_pair(up2, down2)
     own_top4, own_bottom4 = ring_end(own_up3, own_down3)

time: 254 us -> 255 us (level)
    ppermute x1, waiting for transfers between devices: 0.01 us -> 4.35 us  [local(): x_m = lax.ppermute(x_sent, 'section', mirror)]
    all_to_all x1, waiting for transfers between devices: 6.77 us -> 3.13 us  [local(): lax.all_to_all(out_mir, 'dp', split_axis=0, concat_axis=0, tiled=True)]
  transfers between devices with their start and end apart: 27 -> 27, of which waited for: 14 -> 13; matrix products, arithmetic and copies ran while one was open for 5% -> 5% of each run, Pallas kernels for 7% -> 7%
where the time goes in v4:
time: 255 us
  waiting for transfers between devices  139 us (55%)
  starting transfers between devices  60.4 us (24%)
  Pallas kernels  34.3 us (13%)
  other arithmetic  9.73 us (4%)
  local copies, waits for them, and re-layouts  8.4 us (3%)
  between operations  3.01 us (1%)
    ppermute x16, waiting for transfers between devices, z_step(): return lax.ppermute(value, 'dp', pairs)  98.2 us
    ppermute x6, waiting for transfers between devices, x_swap(): return lax.ppermute(value, 'dp', [(d, d ^ 1) for d in range(count)])  31.9 us
    ppermute x16, starting transfers between devices, z_step(): return lax.ppermute(value, 'dp', pairs)  26.5 us
    ppermute x6, starting transfers between devices, x_swap(): return lax.ppermute(value, 'dp', [(d, d ^ 1) for d in range(count)])  16.1 us
    pallas_call x1, Pallas kernels, last_part(): pl.pallas_call(functools.partial(last_kernel, rows, first_late), grid=(wi...  15.8 us
    pallas_call x1, Pallas kernels, first_part(): pl.pallas_call(functools.partial(first_kernel, rows, held), grid=(width /...  11.4 us
    all_to_all x1, starting transfers between devices, local(): lax.all_to_all(out_own, 'dp', split_axis=0, concat_axis=0, tiled=True)  9.75 us
    pallas_call x2, Pallas kernels, route(): pl.pallas_call(functools.partial(route_kernel, inverses is not None, slot...  7.1 us
  transfers between devices with their start and end apart: 27, of which 13 were waited for; matrix products, arithmetic and copies ran while one was open for 5% of the time, Pallas kernels for 7%

profile of v4, /device:TPU:16, one launch (start us, length us, event | category | flops | bytes accessed | tf_op | source)
XLA Modules:
  0.0 254.6 jit_solution(13241079394888684481)
XLA Ops:
  3.8 3.1 %collective-permute-start = (bf16[64,2048]{1,0:T(8,128)(2,1)S(1)}, bf16[64,2048]{1,0:T(8,128)(2,1)S(1)}, u32[]{:S(2)}, u32[]{:S(2)}) collective-permute-start(bf16[64,2048]{1,0:T(8,128)(2,1)S(1)} %bitcast_select_fusion), channel_id=1, source_target_pairs={{0,1},{1,0},{2,3},{3,2},{4,5},{5,4},{6,7},{7,6},{8,9},{9,8},{10,11... | collective-permute-start | bytes 786440 | tf_op jit(solution)/shard_map/ppermute | solution.py:22
  10.1 3.8 %shard_map.85 = bf16[16,192,512]{2,1,0:T(8,128)(2,1)} custom-call(s32[32]{0:T(128)} %select_reduce_fusion.pick, s32[4]{0:T(128)} %compare_select_fusion.5.limit, s32[1]{0:T(128)} %constant.107.clone.1.count, bf16[64,14336]{1,0:T(8,128)(2,1)} %bitcast.38, bf16[2,512,512]{2,1,0:T(8,128)(2,1)} %bitcast.41), custom_call_target="tpu_custom_call" | custom-call | bytes 8388608 | tf_op jit(solution)/shard_map/pallas_call | solution.py:94
  15.4 9.8 %all-to-all-start = ((bf16[16,192,512]{2,1,0:T(8,128)(2,1)}), bf16[16,192,512]{2,1,0:T(8,128)(2,1)S(1)}, u32[]{:S(2)}, u32[]{:S(2)}) async-start(bf16[16,192,512]{2,1,0:T(8,128)(2,1)} %shard_map.85), calls=%async_computation | async-start | bytes 6291456 | tf_op jit(solution)/shard_map/all_to_all | solution.py:340
  35.0 4.4 %collective-permute-done.2 = bf16[64,2048]{1,0:T(8,128)(2,1)S(1)} collective-permute-done((bf16[64,2048]{1,0:T(8,128)(2,1)}, bf16[64,2048]{1,0:T(8,128)(2,1)S(1)}, u32[]{:S(2)}, u32[]{:S(2)}) %collective-permute-start.2) | collective-permute-done | bytes 262176 | tf_op jit(solution)/shard_map/ppermute | solution.py:333
  39.5 67.0 %collective-permute-done.5.refs_1_ = bf16[128,2048]{1,0:T(8,128)(2,1)} collective-permute-done((bf16[128,2048]{1,0:T(8,128)(2,1)S(1)}, bf16[128,2048]{1,0:T(8,128)(2,1)}, u32[]{:S(2)}, u32[]{:S(2)}) %collective-permute-start.5) | collective-permute-done | bytes 524320 | tf_op jit(solution)/shard_map/ppermute | solution.py:17
  113.2 3.2 %collective-permute-start.4 = (bf16[96,2048]{1,0:T(8,128)(2,1)S(1)}, bf16[96,2048]{1,0:T(8,128)(2,1)S(1)}, u32[]{:S(2)}, u32[]{:S(2)}) collective-permute-start(bf16[96,2048]{1,0:T(8,128)(2,1)S(1)} %pad_maximum_fusion.4.refs_0_), channel_id=1, source_target_pairs={{0,14},{1,15},{2,0},{3,1},{4,2},{5,3},{6,4},{7,5},{8,6},{9,7},{10,... | collective-permute-start | bytes 1179656 | tf_op jit(solution)/shard_map/ppermute | solution.py:17
  116.4 6.5 %collective-permute-done.6.refs_2_ = bf16[128,2048]{1,0:T(8,128)(2,1)} collective-permute-done((bf16[128,2048]{1,0:T(8,128)(2,1)}, bf16[128,2048]{1,0:T(8,128)(2,1)}, u32[]{:S(2)}, u32[]{:S(2)}) %collective-permute-start.6) | collective-permute-done | bytes 524320 | tf_op jit(solution)/shard_map/ppermute | solution.py:17
  122.9 3.0 %collective-permute-start.14 = (bf16[96,2048]{1,0:T(8,128)(2,1)S(1)}, bf16[96,2048]{1,0:T(8,128)(2,1)S(1)}, u32[]{:S(2)}, u32[]{:S(2)}) collective-permute-start(bf16[96,2048]{1,0:T(8,128)(2,1)S(1)} %pad_maximum_fusion.4.refs_0_), channel_id=1, source_target_pairs={{0,1},{1,0},{2,3},{3,2},{4,5},{5,4},{6,7},{7,6},{8,9},{9,8},{10,11... | collective-permute-start | bytes 1179656 | tf_op jit(solution)/shard_map/ppermute | solution.py:22
  125.9 3.1 %collective-permute-done.3.refs_1_ = bf16[96,2048]{1,0:T(8,128)(2,1)S(1)} collective-permute-done((bf16[96,2048]{1,0:T(8,128)(2,1)S(1)}, bf16[96,2048]{1,0:T(8,128)(2,1)S(1)}, u32[]{:S(2)}, u32[]{:S(2)}) %collective-permute-start.3) | collective-permute-done | bytes 393248 | tf_op jit(solution)/shard_map/ppermute | solution.py:17
  129.4 2.9 %collective-permute-start.13 = (bf16[128,2048]{1,0:T(8,128)(2,1)}, bf16[128,2048]{1,0:T(8,128)(2,1)}, u32[]{:S(2)}, u32[]{:S(2)}) collective-permute-start(bf16[128,2048]{1,0:T(8,128)(2,1)} %collective-permute-done.8.refs_7_), channel_id=1, source_target_pairs={{0,14},{1,15},{2,0},{3,1},{4,2},{5,3},{6,4},{7,5},{8,6},{9,7},{10,... | collective-permute-start | bytes 1572872 | tf_op jit(solution)/shard_map/ppermute | solution.py:17
  132.3 3.2 %collective-permute-start.11 = (bf16[96,2048]{1,0:T(8,128)(2,1)S(1)}, bf16[96,2048]{1,0:T(8,128)(2,1)S(1)}, u32[]{:S(2)}, u32[]{:S(2)}) collective-permute-start(bf16[96,2048]{1,0:T(8,128)(2,1)S(1)} %collective-permute-done.4.refs_8_), channel_id=1, source_target_pairs={{0,14},{1,15},{2,0},{3,1},{4,2},{5,3},{6,4},{7,5},{8,6},{9,7},{10,... | collective-permute-start | bytes 1179656 | tf_op jit(solution)/shard_map/ppermute | solution.py:17
  135.6 3.1 %collective-permute-start.19 = (bf16[192,2048]{1,0:T(8,128)(2,1)S(1)}, bf16[192,2048]{1,0:T(8,128)(2,1)}, u32[]{:S(2)}, u32[]{:S(2)}) collective-permute-start(bf16[192,2048]{1,0:T(8,128)(2,1)S(1)} %pad_maximum_fusion), channel_id=1, source_target_pairs={{0,1},{1,0},{2,3},{3,2},{4,5},{5,4},{6,7},{7,6},{8,9},{9,8},{10,11... | collective-permute-start | bytes 2359304 | tf_op jit(solution)/shard_map/ppermute | solution.py:22
  139.9 3.3 %shard_map.86 = bf16[16,144,512]{2,1,0:T(8,128)(2,1)} custom-call(s32[32]{0:T(128)} %select_reduce_fusion.pick, s32[4]{0:T(128)} %get-tuple-element.69.limit, s32[1]{0:T(128)} %bitcast.20.count, bf16[64,14336]{1,0:T(8,128)(2,1)} %collective-permute-done.9.g_ref), custom_call_target="tpu_custom_call" | custom-call | bytes 8388608 | tf_op jit(solution)/shard_map/pallas_call | solution.py:94
  143.2 7.4 %collective-permute-done.10.refs_2_ = bf16[96,2048]{1,0:T(8,128)(2,1)S(1)} collective-permute-done((bf16[96,2048]{1,0:T(8,128)(2,1)S(1)}, bf16[96,2048]{1,0:T(8,128)(2,1)S(1)}, u32[]{:S(2)}, u32[]{:S(2)}) %collective-permute-start.10) | collective-permute-done | bytes 393248 | tf_op jit(solution)/shard_map/ppermute | solution.py:17
  150.6 3.2 %collective-permute-start.22 = (bf16[192,2048]{1,0:T(8,128)(2,1)S(1)}, bf16[192,2048]{1,0:T(8,128)(2,1)}, u32[]{:S(2)}, u32[]{:S(2)}) collective-permute-start(bf16[192,2048]{1,0:T(8,128)(2,1)S(1)} %pad_maximum_fusion.1), channel_id=1, source_target_pairs={{0,1},{1,0},{2,3},{3,2},{4,5},{5,4},{6,7},{7,6},{8,9},{9,8},{10,11... | collective-permute-start | bytes 2359304 | tf_op jit(solution)/shard_map/ppermute | solution.py:22
  153.9 3.7 %collective-permute-start.15 = (bf16[96,2048]{1,0:T(8,128)(2,1)S(1)}, bf16[96,2048]{1,0:T(8,128)(2,1)S(1)}, u32[]{:S(2)}, u32[]{:S(2)}) collective-permute-start(bf16[96,2048]{1,0:T(8,128)(2,1)S(1)} %collective-permute-done.10.refs_2_), channel_id=1, source_target_pairs={{0,2},{1,3},{2,4},{3,5},{4,6},{5,7},{6,8},{7,9},{8,10},{9,11},{10,... | collective-permute-start | bytes 1179656 | tf_op jit(solution)/shard_map/ppermute | solution.py:17
  162.0 7.5 %collective-permute-done.17.refs_4_ = bf16[64,2048]{1,0:T(8,128)(2,1)S(1)} collective-permute-done((bf16[64,2048]{1,0:T(8,128)(2,1)S(1)}, bf16[64,2048]{1,0:T(8,128)(2,1)S(1)}, u32[]{:S(2)}, u32[]{:S(2)}) %collective-permute-start.17) | collective-permute-done | bytes 262176 | tf_op jit(solution)/shard_map/ppermute | solution.py:17
  175.2 3.5 %collective-permute-done.20.refs_4_ = bf16[48,2048]{1,0:T(8,128)(2,1)S(1)} collective-permute-done((bf16[48,2048]{1,0:T(8,128)(2,1)S(1)}, bf16[48,2048]{1,0:T(8,128)(2,1)S(1)}, u32[]{:S(2)}, u32[]{:S(2)}) %collective-permute-start.20) | collective-permute-done | bytes 196640 | tf_op jit(solution)/shard_map/ppermute | solution.py:17
  179.4 5.3 %all-to-all-start.1 = ((bf16[16,144,512]{2,1,0:T(8,128)(2,1)}), bf16[16,144,512]{2,1,0:T(8,128)(2,1)S(1)}, u32[]{:S(2)}, u32[]{:S(2)}) async-start(bf16[16,144,512]{2,1,0:T(8,128)(2,1)} %shard_map.86), calls=%async_computation.1 | async-start | bytes 4718592 | tf_op jit(solution)/shard_map/all_to_all | solution.py:367
  186.3 3.5 %collective-permute-start.23 = (bf16[192,2048]{1,0:T(8,128)(2,1)S(1)}, bf16[192,2048]{1,0:T(8,128)(2,1)S(1)}, u32[]{:S(2)}, u32[]{:S(2)}) collective-permute-start(bf16[192,2048]{1,0:T(8,128)(2,1)S(1)} %pad_maximum_fusion.2), channel_id=1, source_target_pairs={{0,1},{1,0},{2,3},{3,2},{4,5},{5,4},{6,7},{7,6},{8,9},{9,8},{10,11... | collective-permute-start | bytes 2359304 | tf_op jit(solution)/shard_map/ppermute | solution.py:22
  190.8 11.4 %shard_map.87 = (f32[2,512,2048]{2,1,0:T(8,128)}, f32[2,512,256]{2,1,0:T(8,128)}, f32[128,512]{1,0:T(8,128)}) custom-call(s32[16]{0:T(128)} %add.90.source, s32[4]{0:T(128)} %pad_add_fusion.1.place, bf16[16,192,512]{2,1,0:T(8,128)(2,1)} %copy-done, bf16[128,2048]{1,0:T(8,128)(2,1)} %copy-done.5, bf16[128,2048]{1,0:T(8,128)(2,1)} %collective-permute-done.5.refs_1_, ...), custom_call_target="tpu_custom_call" | custom-call | flops 4831838208 | bytes 16777216 | tf_op jit(solution)/shard_map/pallas_call | solution.py:175
  202.2 31.9 %collective-permute-done.24.refs_13_ = bf16[96,2048]{1,0:T(8,128)(2,1)S(1)} collective-permute-done((bf16[96,2048]{1,0:T(8,128)(2,1)S(1)}, bf16[96,2048]{1,0:T(8,128)(2,1)S(1)}, u32[]{:S(2)}, u32[]{:S(2)}) %collective-permute-start.24) | collective-permute-done | bytes 393248 | tf_op jit(solution)/shard_map/ppermute | solution.py:22
  234.1 3.1 %all-to-all-done.1.routed_ref = bf16[16,144,512]{2,1,0:T(8,128)(2,1)S(1)} async-done(((bf16[16,144,512]{2,1,0:T(8,128)(2,1)}), bf16[16,144,512]{2,1,0:T(8,128)(2,1)S(1)}, u32[]{:S(2)}, u32[]{:S(2)}) %all-to-all-start.1) | async-done | bytes 2359328 | tf_op jit(solution)/shard_map/all_to_all | solution.py:367
  238.7 15.8 %shard_map.88 = (bf16[2,512,2048]{2,1,0:T(8,128)(2,1)}, bf16[2,512,256]{2,1,0:T(8,128)(2,1)}, f32[128,512]{1,0:T(8,128)}) custom-call(s32[16]{0:T(128)} %add.90.source, s32[4]{0:T(128)} %pad_add_fusion.1.place, s32[2]{0:T(128)} %convert_element_type.13.used, bf16[16,144,512]{2,1,0:T(8,128)(2,1)} %copy-done.1, bf16[96,2048]{1,0:T(8,128)(2,1)} %copy-done.6, ...), custom_call_target="tpu_custom_call" | custom-call | flops 8589934592 | bytes 25165824 | tf_op jit(solution)/shard_map/pallas_call | solution.py:260
  (114 shorter events, 39.0 us)
Async XLA Ops:
  3.8 10.9 %collective-permute-start = (bf16[64,2048]{1,0:T(8,128)(2,1)S(1)}, bf16[64,2048]{1,0:T(8,128)(2,1)S(1)}, u32[]{:S(2)}, u32[]{:S(2)}) collective-permute-start(bf16[64,2048]{1,0:T(8,128)(2,1)S(1)} %bitcast_select_fusion), channel_id=1, source_target_pairs={{0,1},{1,0},{2,3},{3,2},{4,5},{5,4},{6,7},{7,6},{8,9},{9,8},{10,11... | collective-permute-start | bytes 786440 | tf_op jit(solution)/shard_map/ppermute | solution.py:22
  15.4 94.4 %all-to-all-start = ((bf16[16,192,512]{2,1,0:T(8,128)(2,1)}), bf16[16,192,512]{2,1,0:T(8,128)(2,1)S(1)}, u32[]{:S(2)}, u32[]{:S(2)}) async-start(bf16[16,192,512]{2,1,0:T(8,128)(2,1)} %shard_map.85), calls=%async_computation | async-start | bytes 6291456 | tf_op jit(solution)/shard_map/all_to_all | solution.py:340
  26.3 80.2 %collective-permute-start.5 = (bf16[128,2048]{1,0:T(8,128)(2,1)S(1)}, bf16[128,2048]{1,0:T(8,128)(2,1)}, u32[]{:S(2)}, u32[]{:S(2)}) collective-permute-start(bf16[128,2048]{1,0:T(8,128)(2,1)S(1)} %pad_maximum_fusion.3.refs_0_), channel_id=1, source_target_pairs={{0,2},{1,3},{2,4},{3,5},{4,6},{5,7},{6,8},{7,9},{8,10},{9,11},{10,... | collective-permute-start | bytes 1572872 | tf_op jit(solution)/shard_map/ppermute | solution.py:17
  28.3 78.5 %collective-permute-start.7 = (bf16[128,2048]{1,0:T(8,128)(2,1)S(1)}, bf16[128,2048]{1,0:T(8,128)(2,1)}, u32[]{:S(2)}, u32[]{:S(2)}) collective-permute-start(bf16[128,2048]{1,0:T(8,128)(2,1)S(1)} %pad_maximum_fusion.3.refs_0_), channel_id=1, source_target_pairs={{0,14},{1,15},{2,0},{3,1},{4,2},{5,3},{6,4},{7,5},{8,6},{9,7},{10,... | collective-permute-start | bytes 1572872 | tf_op jit(solution)/shard_map/ppermute | solution.py:17
  29.6 9.7 %collective-permute-start.2 = (bf16[64,2048]{1,0:T(8,128)(2,1)}, bf16[64,2048]{1,0:T(8,128)(2,1)S(1)}, u32[]{:S(2)}, u32[]{:S(2)}) collective-permute-start(bf16[64,2048]{1,0:T(8,128)(2,1)} %dynamic-slice_bitcast_fusion), channel_id=1, source_target_pairs={{0,240},{16,224},{32,208},{48,192},{64,176},{80,160},{96,144},{112... | collective-permute-start | bytes 786440 | tf_op jit(solution)/shard_map/ppermute | solution.py:333
  32.3 93.6 %collective-permute-start.9 = (bf16[64,14336]{1,0:T(8,128)(2,1)}, bf16[64,14336]{1,0:T(8,128)(2,1)}, u32[]{:S(2)}, u32[]{:S(2)}) collective-permute-start(bf16[64,14336]{1,0:T(8,128)(2,1)} %bitcast.39), channel_id=1, source_target_pairs={{0,240},{16,224},{32,208},{48,192},{64,176},{80,160},{96,144},{112... | collective-permute-start | bytes 5505032 | tf_op jit(solution)/shard_map/ppermute | solution.py:334
  106.5 16.4 %collective-permute-start.6 = (bf16[128,2048]{1,0:T(8,128)(2,1)}, bf16[128,2048]{1,0:T(8,128)(2,1)}, u32[]{:S(2)}, u32[]{:S(2)}) collective-permute-start(bf16[128,2048]{1,0:T(8,128)(2,1)} %collective-permute-done.5.refs_1_), channel_id=1, source_target_pairs={{0,2},{1,3},{2,4},{3,5},{4,6},{5,7},{6,8},{7,9},{8,10},{9,11},{10,... | collective-permute-start | bytes 1572872 | tf_op jit(solution)/shard_map/ppermute | solution.py:17
  106.9 19.0 %collective-permute-start.8 = (bf16[128,2048]{1,0:T(8,128)(2,1)}, bf16[128,2048]{1,0:T(8,128)(2,1)}, u32[]{:S(2)}, u32[]{:S(2)}) collective-permute-start(bf16[128,2048]{1,0:T(8,128)(2,1)} %collective-permute-done.7.refs_8_), channel_id=1, source_target_pairs={{0,14},{1,15},{2,0},{3,1},{4,2},{5,3},{6,4},{7,5},{8,6},{9,7},{10,... | collective-permute-start | bytes 1572872 | tf_op jit(solution)/shard_map/ppermute | solution.py:17
  113.1 15.8 %collective-permute-start.3 = (bf16[96,2048]{1,0:T(8,128)(2,1)S(1)}, bf16[96,2048]{1,0:T(8,128)(2,1)S(1)}, u32[]{:S(2)}, u32[]{:S(2)}) collective-permute-start(bf16[96,2048]{1,0:T(8,128)(2,1)S(1)} %pad_maximum_fusion.4.refs_0_), channel_id=1, source_target_pairs={{0,2},{1,3},{2,4},{3,5},{4,6},{5,7},{6,8},{7,9},{8,10},{9,11},{10,... | collective-permute-start | bytes 1179656 | tf_op jit(solution)/shard_map/ppermute | solution.py:17
  113.2 15.7 %collective-permute-start.4 = (bf16[96,2048]{1,0:T(8,128)(2,1)S(1)}, bf16[96,2048]{1,0:T(8,128)(2,1)S(1)}, u32[]{:S(2)}, u32[]{:S(2)}) collective-permute-start(bf16[96,2048]{1,0:T(8,128)(2,1)S(1)} %pad_maximum_fusion.4.refs_0_), channel_id=1, source_target_pairs={{0,14},{1,15},{2,0},{3,1},{4,2},{5,3},{6,4},{7,5},{8,6},{9,7},{10,... | collective-permute-start | bytes 1179656 | tf_op jit(solution)/shard_map/ppermute | solution.py:17
  122.9 12.7 %collective-permute-start.14 = (bf16[96,2048]{1,0:T(8,128)(2,1)S(1)}, bf16[96,2048]{1,0:T(8,128)(2,1)S(1)}, u32[]{:S(2)}, u32[]{:S(2)}) collective-permute-start(bf16[96,2048]{1,0:T(8,128)(2,1)S(1)} %pad_maximum_fusion.4.refs_0_), channel_id=1, source_target_pairs={{0,1},{1,0},{2,3},{3,2},{4,5},{5,4},{6,7},{7,6},{8,9},{9,8},{10,11... | collective-permute-start | bytes 1179656 | tf_op jit(solution)/shard_map/ppermute | solution.py:22
  128.9 21.6 %collective-permute-start.12 = (bf16[128,2048]{1,0:T(8,128)(2,1)}, bf16[128,2048]{1,0:T(8,128)(2,1)S(1)}, u32[]{:S(2)}, u32[]{:S(2)}) collective-permute-start(bf16[128,2048]{1,0:T(8,128)(2,1)} %collective-permute-done.6.refs_2_), channel_id=1, source_target_pairs={{0,2},{1,3},{2,4},{3,5},{4,6},{5,7},{6,8},{7,9},{8,10},{9,11},{10,... | collective-permute-start | bytes 1572872 | tf_op jit(solution)/shard_map/ppermute | solution.py:17
  129.4 21.2 %collective-permute-start.13 = (bf16[128,2048]{1,0:T(8,128)(2,1)}, bf16[128,2048]{1,0:T(8,128)(2,1)}, u32[]{:S(2)}, u32[]{:S(2)}) collective-permute-start(bf16[128,2048]{1,0:T(8,128)(2,1)} %collective-permute-done.8.refs_7_), channel_id=1, source_target_pairs={{0,14},{1,15},{2,0},{3,1},{4,2},{5,3},{6,4},{7,5},{8,6},{9,7},{10,... | collective-permute-start | bytes 1572872 | tf_op jit(solution)/shard_map/ppermute | solution.py:17
  132.3 18.3 %collective-permute-start.10 = (bf16[96,2048]{1,0:T(8,128)(2,1)S(1)}, bf16[96,2048]{1,0:T(8,128)(2,1)S(1)}, u32[]{:S(2)}, u32[]{:S(2)}) collective-permute-start(bf16[96,2048]{1,0:T(8,128)(2,1)S(1)} %collective-permute-done.3.refs_1_), channel_id=1, source_target_pairs={{0,2},{1,3},{2,4},{3,5},{4,6},{5,7},{6,8},{7,9},{8,10},{9,11},{10,... | collective-permute-start | bytes 1179656 | tf_op jit(solution)/shard_map/ppermute | solution.py:17
  132.3 18.3 %collective-permute-start.11 = (bf16[96,2048]{1,0:T(8,128)(2,1)S(1)}, bf16[96,2048]{1,0:T(8,128)(2,1)S(1)}, u32[]{:S(2)}, u32[]{:S(2)}) collective-permute-start(bf16[96,2048]{1,0:T(8,128)(2,1)S(1)} %collective-permute-done.4.refs_8_), channel_id=1, source_target_pairs={{0,14},{1,15},{2,0},{3,1},{4,2},{5,3},{6,4},{7,5},{8,6},{9,7},{10,... | collective-permute-start | bytes 1179656 | tf_op jit(solution)/shard_map/ppermute | solution.py:17
  135.6 25.1 %collective-permute-start.19 = (bf16[192,2048]{1,0:T(8,128)(2,1)S(1)}, bf16[192,2048]{1,0:T(8,128)(2,1)}, u32[]{:S(2)}, u32[]{:S(2)}) collective-permute-start(bf16[192,2048]{1,0:T(8,128)(2,1)S(1)} %pad_maximum_fusion), channel_id=1, source_target_pairs={{0,1},{1,0},{2,3},{3,2},{4,5},{5,4},{6,7},{7,6},{8,9},{9,8},{10,11... | collective-permute-start | bytes 2359304 | tf_op jit(solution)/shard_map/ppermute | solution.py:22
  150.6 28.8 %collective-permute-start.22 = (bf16[192,2048]{1,0:T(8,128)(2,1)S(1)}, bf16[192,2048]{1,0:T(8,128)(2,1)}, u32[]{:S(2)}, u32[]{:S(2)}) collective-permute-start(bf16[192,2048]{1,0:T(8,128)(2,1)S(1)} %pad_maximum_fusion.1), channel_id=1, source_target_pairs={{0,1},{1,0},{2,3},{3,2},{4,5},{5,4},{6,7},{7,6},{8,9},{9,8},{10,11... | collective-permute-start | bytes 2359304 | tf_op jit(solution)/shard_map/ppermute | solution.py:22
  153.9 17.8 %collective-permute-start.15 = (bf16[96,2048]{1,0:T(8,128)(2,1)S(1)}, bf16[96,2048]{1,0:T(8,128)(2,1)S(1)}, u32[]{:S(2)}, u32[]{:S(2)}) collective-permute-start(bf16[96,2048]{1,0:T(8,128)(2,1)S(1)} %collective-permute-done.10.refs_2_), channel_id=1, source_target_pairs={{0,2},{1,3},{2,4},{3,5},{4,6},{5,7},{6,8},{7,9},{8,10},{9,11},{10,... | collective-permute-start | bytes 1179656 | tf_op jit(solution)/shard_map/ppermute | solution.py:17
  157.6 14.1 %collective-permute-start.16 = (bf16[96,2048]{1,0:T(8,128)(2,1)S(1)}, bf16[96,2048]{1,0:T(8,128)(2,1)S(1)}, u32[]{:S(2)}, u32[]{:S(2)}) collective-permute-start(bf16[96,2048]{1,0:T(8,128)(2,1)S(1)} %collective-permute-done.11.refs_7_), channel_id=1, source_target_pairs={{0,14},{1,15},{2,0},{3,1},{4,2},{5,3},{6,4},{7,5},{8,6},{9,7},{10,... | collective-permute-start | bytes 1179656 | tf_op jit(solution)/shard_map/ppermute | solution.py:17
  157.6 11.9 %collective-permute-start.17 = (bf16[64,2048]{1,0:T(8,128)(2,1)S(1)}, bf16[64,2048]{1,0:T(8,128)(2,1)S(1)}, u32[]{:S(2)}, u32[]{:S(2)}) collective-permute-start(bf16[64,2048]{1,0:T(8,128)(2,1)S(1)} %slice.42), channel_id=1, source_target_pairs={{0,2},{1,3},{2,4},{3,5},{4,6},{5,7},{6,8},{7,9},{8,10},{9,11},{10,... | collective-permute-start | bytes 786440 | tf_op jit(solution)/shard_map/ppermute | solution.py:17
  160.7 11.0 %collective-permute-start.18 = (bf16[64,2048]{1,0:T(8,128)(2,1)S(1)}, bf16[64,2048]{1,0:T(8,128)(2,1)S(1)}, u32[]{:S(2)}, u32[]{:S(2)}) collective-permute-start(bf16[64,2048]{1,0:T(8,128)(2,1)S(1)} %slice.43), channel_id=1, source_target_pairs={{0,14},{1,15},{2,0},{3,1},{4,2},{5,3},{6,4},{7,5},{8,6},{9,7},{10,... | collective-permute-start | bytes 786440 | tf_op jit(solution)/shard_map/ppermute | solution.py:17
  179.4 57.8 %all-to-all-start.1 = ((bf16[16,144,512]{2,1,0:T(8,128)(2,1)}), bf16[16,144,512]{2,1,0:T(8,128)(2,1)S(1)}, u32[]{:S(2)}, u32[]{:S(2)}) async-start(bf16[16,144,512]{2,1,0:T(8,128)(2,1)} %shard_map.86), calls=%async_computation.1 | async-start | bytes 4718592 | tf_op jit(solution)/shard_map/all_to_all | solution.py:367
  186.3 47.8 %collective-permute-start.23 = (bf16[192,2048]{1,0:T(8,128)(2,1)S(1)}, bf16[192,2048]{1,0:T(8,128)(2,1)S(1)}, u32[]{:S(2)}, u32[]{:S(2)}) collective-permute-start(bf16[192,2048]{1,0:T(8,128)(2,1)S(1)} %pad_maximum_fusion.2), channel_id=1, source_target_pairs={{0,1},{1,0},{2,3},{3,2},{4,5},{5,4},{6,7},{7,6},{8,9},{9,8},{10,11... | collective-permute-start | bytes 2359304 | tf_op jit(solution)/shard_map/ppermute | solution.py:22
  190.5 43.6 %collective-permute-start.24 = (bf16[96,2048]{1,0:T(8,128)(2,1)S(1)}, bf16[96,2048]{1,0:T(8,128)(2,1)S(1)}, u32[]{:S(2)}, u32[]{:S(2)}) collective-permute-start(bf16[96,2048]{1,0:T(8,128)(2,1)S(1)} %pad_maximum_fusion.5), channel_id=1, source_target_pairs={{0,1},{1,0},{2,3},{3,2},{4,5},{5,4},{6,7},{7,6},{8,9},{9,8},{10,11... | collective-permute-start | bytes 1179656 | tf_op jit(solution)/shard_map/ppermute | solution.py:22
  (24 other events, 323.9 us)
